TPU v7x, 128 devices: a whole 4x4x4 slice. The times are simulated.
128 devices in a mesh: row: 4 (over x_hi, core), col: 32 (over y, z, x_lo).
Axes of the slice: x: 4 (x_hi: 2, x_lo: 2; x = x_hi * 2 + x_lo), y: 4, z: 4, core: 2. Of those that a mesh axis runs over, the one named last changes fastest.
Arguments:
- force: bfloat16 [3, 256, 256, 512], P(None, 'col', 'row'), may hold values from -6 to 6
- mask: int32 [256, 256, 512], P('col', 'row'), may hold values from 0 to 1, as said below
- scalar: bfloat16 [256, 256, 512], P('col', 'row'), may hold values from -9 to 9
Outputs:
- velocity: bfloat16 [3, 256, 256, 512], P(None, 'col', 'row')
- concentration: bfloat16 [256, 256, 512], P('col', 'row')
Inputs may be any that keep to these rules, and one draw needn't show every extreme that they name: `mask`: 1 marks a solid cell and 0 a fluid one.
All inputs are finite; a program needn't handle non-finite values.
Results may differ from a plain program's by a relative error of at most 0.029.
Values may be sent and summed in bfloat16 or wider, within the bound.
A program may use at most 64 MiB of HBM per device.

v0:
```python
import math

import jax
import jax.numpy as jnp
from jax import lax
from jax.sharding import PartitionSpec as P

NX = 512
NY = 256
NZ = 256
SECTIONS = 5


viscosity = 0.05
damping = 0.5
penalty = 1.0
time_step = 0.25
diffusivity = 0.25


def extended(value, sides, width):
    for axis, dim in sides:
        devices, length = (lax.axis_size(axis), value.shape[dim])
        up = [(i, (i + 1) % devices) for i in range(devices)]
        down = [(j, i) for i, j in up]
        last = lax.slice_in_dim(value, length - width, length, axis=dim)
        initial = lax.slice_in_dim(value, 0, width, axis=dim)
        before = lax.ppermute(last, axis, up)
        after = lax.ppermute(initial, axis, down)
        value = jnp.concatenate([before, value, after], axis=dim)
    return value


def phases(rows_index, cols_index, length):
    product = rows_index[:, None] * cols_index[None, :] % length
    return product.astype(jnp.float32) * (2.0 * math.pi / length)


def square_tables(length):
    places = jnp.arange(length, dtype=jnp.int32)
    angles = phases(places, places, length)
    scaling = 1.0 / math.sqrt(length)
    return (
        (jnp.cos(angles) * scaling).astype(jnp.bfloat16),
        (jnp.sin(angles) * scaling).astype(jnp.bfloat16),
    )


def wavenumber(index, length):
    signed = jnp.where(index < length // 2, index, index - length)
    return (signed.astype(jnp.float32) * (2.0 * math.pi / length), index == length // 2)


def line_tables(groups, mode_count, weight):
    per_group = mode_count // groups
    places = jnp.arange(NX, dtype=jnp.int32)
    frequencies = jnp.arange(mode_count, dtype=jnp.int32)
    scaling = 1.0 / math.sqrt(NX)
    angles = phases(places, frequencies, NX)
    forward_cos = (jnp.cos(angles) * scaling).reshape(NX, groups, per_group)
    forward_sin = (-(jnp.sin(angles) * scaling)).reshape(NX, groups, per_group)
    forward_table = (
        jnp.stack([forward_cos, forward_sin], axis=2)
        .reshape(NX, groups * 2 * per_group)
        .astype(jnp.bfloat16)
    )
    back_angles = phases(frequencies, places, NX)
    back_cos = (weight[:, None] * jnp.cos(back_angles) * scaling).reshape(groups, per_group, NX)
    back_sin = (-(weight[:, None] * jnp.sin(back_angles) * scaling)).reshape(groups, per_group, NX)
    backward_table = (
        jnp.stack([back_cos, back_sin], axis=1)
        .reshape(groups * 2 * per_group, NX)
        .astype(jnp.bfloat16)
    )
    return (forward_table, backward_table)


def spectral_factors(mode_count):
    per_row = mode_count // lax.axis_size("row")
    per_col = NY // lax.axis_size("col")
    index_x = lax.axis_index("row") * per_row + jnp.arange(per_row, dtype=jnp.int32)
    index_y = lax.axis_index("col") * per_col + jnp.arange(per_col, dtype=jnp.int32)
    index_z = jnp.arange(NZ, dtype=jnp.int32)
    wave_x, nyquist_x = wavenumber(index_x, NX)
    wave_y, nyquist_y = wavenumber(index_y, NY)
    wave_z, nyquist_z = wavenumber(index_z, NZ)
    wave_x = wave_x[None, None, :]
    wave_y = wave_y[None, :, None]
    wave_z = wave_z[:, None, None]
    shape_all = (NZ, per_col, per_row)
    ksq = wave_x * wave_x + wave_y * wave_y + wave_z * wave_z
    nyquist = nyquist_x[None, None, :] | nyquist_y[None, :, None] | nyquist_z[:, None, None]
    damping_gain = jnp.where(nyquist, 0.0, 1.0 / (viscosity * ksq + damping))
    inverse_sq = jnp.where(ksq > 0.0, 1.0 / jnp.where(ksq > 0.0, ksq, 1.0), 0.0)
    wave_vector = jnp.stack(
        [
            jnp.broadcast_to(wave_x, shape_all),
            jnp.broadcast_to(wave_y, shape_all),
            jnp.broadcast_to(wave_z, shape_all),
        ]
    )

    def doubled(values):
        return jnp.concatenate([values, values], axis=-1)

    return (doubled(wave_vector), doubled(damping_gain), doubled(inverse_sq))


def project(vector_field, wave_vector, damping_gain, inverse_sq):
    along_wave = (
        wave_vector[0] * vector_field[0]
        + wave_vector[1] * vector_field[1]
        + wave_vector[2] * vector_field[2]
    )
    return damping_gain * (vector_field - wave_vector * (along_wave * inverse_sq))


def pair_pass(spectra, cosine, sine, pattern, orientation):
    middle = spectra.shape[-1] // 2
    with_cos = jnp.einsum(pattern, cosine, spectra, preferred_element_type=jnp.float32)
    with_sin = jnp.einsum(pattern, sine, spectra, preferred_element_type=jnp.float32)
    new_real = with_cos[..., :middle] + orientation * with_sin[..., middle:]
    new_imag = with_cos[..., middle:] - orientation * with_sin[..., :middle]
    return jnp.concatenate([new_real, new_imag], axis=-1).astype(jnp.bfloat16)


def forward(values, forward_table, y_tables, z_tables):
    spread = jnp.dot(values, forward_table, preferred_element_type=jnp.float32).astype(jnp.bfloat16)
    spread = lax.all_to_all(spread, "row", split_axis=3, concat_axis=2, tiled=True)
    spread = pair_pass(spread, y_tables[0], y_tables[1], "qy,czyk->czqk", 1.0)
    spread = lax.all_to_all(spread, "col", split_axis=2, concat_axis=1, tiled=True)
    return pair_pass(spread, z_tables[0], z_tables[1], "qz,czyk->cqyk", 1.0)


def backward(spectra, backward_table, y_tables, z_tables):
    spread = pair_pass(spectra, z_tables[0], z_tables[1], "qz,czyk->cqyk", -1.0)
    spread = lax.all_to_all(spread, "col", split_axis=1, concat_axis=2, tiled=True)
    spread = pair_pass(spread, y_tables[0], y_tables[1], "qy,czyk->czqk", -1.0)
    spread = lax.all_to_all(spread, "row", split_axis=2, concat_axis=3, tiled=True)
    return jnp.dot(spread, backward_table, preferred_element_type=jnp.float32).astype(jnp.bfloat16)


def flux_term(center, lower_cell, upper_cell, speed):
    return diffusivity * (upper_cell + lower_cell - 2.0 * center) - (
        jnp.maximum(speed, 0.0) * (center - lower_cell)
        + jnp.minimum(speed, 0.0) * (upper_cell - center)
    )


def advance(padded, speeds, fluid_cells):
    center = padded[1:-1, 1:-1]
    summed = flux_term(center, jnp.roll(center, 1, 2), jnp.roll(center, -1, 2), speeds[0])
    summed = summed + flux_term(center, padded[1:-1, :-2], padded[1:-1, 2:], speeds[1])
    summed = summed + flux_term(center, padded[:-2, 1:-1], padded[2:, 1:-1], speeds[2])
    return center + time_step * fluid_cells * summed


def scalar_rims(stack, halo_width):
    return extended(stack.astype(jnp.bfloat16), (("row", 2), ("col", 1)), halo_width).astype(
        stack.dtype
    )


def transport(scalar, velocity, mask):
    scalar_state = scalar.astype(jnp.float32)
    fluid_cells = 1.0 - mask.astype(jnp.float32)
    speeds = velocity.astype(jnp.float32)
    for section_index in range(SECTIONS):
        padded = scalar_rims(scalar_state[None], 1)[0]
        scalar_state = advance(padded, speeds, fluid_cells)
    return scalar_state.astype(jnp.bfloat16)


def local(force, mask, scalar):
    row_count = lax.axis_size("row")
    mode_count = NX // 2
    weight = jnp.where(
        jnp.arange(mode_count, dtype=jnp.int32) == 0, jnp.float32(1.0), jnp.float32(2.0)
    )
    forward_table, backward_table = line_tables(row_count, mode_count, weight)
    y_tables = square_tables(NY)
    z_tables = square_tables(NZ)
    wave_vector, damping_gain, inverse_sq = spectral_factors(mode_count)
    force_hat = forward(force, forward_table, y_tables, z_tables)
    first_hat = project(
        force_hat.astype(jnp.float32), wave_vector, damping_gain, inverse_sq
    ).astype(jnp.bfloat16)
    first_pass = backward(first_hat, backward_table, y_tables, z_tables)
    pushed = first_pass * mask.astype(jnp.bfloat16)[None]
    pushed_hat = forward(pushed, forward_table, y_tables, z_tables)
    second_hat = (
        first_hat.astype(jnp.float32)
        - penalty * project(pushed_hat.astype(jnp.float32), wave_vector, damping_gain, inverse_sq)
    ).astype(jnp.bfloat16)
    velocity = backward(second_hat, backward_table, y_tables, z_tables)
    concentration = transport(scalar, velocity, mask)
    return (velocity, concentration)


def solution(mesh):
    placed = (P(None, "col", "row", None), P("col", "row", None), P("col", "row", None))
    return jax.shard_map(
        local,
        mesh=mesh,
        in_specs=placed,
        out_specs=(P(None, "col", "row", None), P("col", "row", None)),
        check_vma=False,
    )
```

profile of v0, /device:TPU:0, one launch (start us, length us, event | category | flops | bytes accessed | tf_op | source)
XLA Modules:
  0.0 435.7 jit_solution(14469307808860705286)
XLA Ops:
  6.2 3.9 copy.75
  10.1 3.3 reshape.448
  13.4 4.4 %all-to-all-start = ((bf16[4,2,98304]{2,1,0:T(2,128)(2,1)}), bf16[4,2,98304]{2,1,0:T(2,128)(2,1)}, u32[]{:S(2)}, u32[]{:S(2)}) async-start(bf16[4,2,98304]{2,1,0:T(2,128)(2,1)} %reshape.448), calls=%async_computation | async-start | bytes 3145728 | tf_op jit(solution)/shard_map/all_to_all | solution.py:129
  17.8 21.6 %all-to-all-done = bf16[4,2,98304]{2,1,0:T(2,128)(2,1)} async-done(((bf16[4,2,98304]{2,1,0:T(2,128)(2,1)}), bf16[4,2,98304]{2,1,0:T(2,128)(2,1)}, u32[]{:S(2)}, u32[]{:S(2)}) %all-to-all-start) | async-done | bytes 1572896 | tf_op jit(solution)/shard_map/all_to_all | solution.py:129
  39.4 3.8 reshape.449
  43.2 3.5 copy.126
  54.5 9.6 %all-to-all-start.1 = ((bf16[3,8,256,128]{3,1,0,2:T(8,128)(2,1)}), bf16[3,8,256,128]{3,1,0,2:T(8,128)(2,1)}, u32[]{:S(2)}, u32[]{:S(2)}) async-start(bf16[3,8,256,128]{3,1,0,2:T(8,128)(2,1)} %copy.80), calls=%async_computation.1 | async-start | bytes 3145728 | tf_op jit(solution)/shard_map/all_to_all | solution.py:131
  67.9 20.5 %all-to-all-done.1 = bf16[3,8,256,128]{3,1,0,2:T(8,128)(2,1)} async-done(((bf16[3,8,256,128]{3,1,0,2:T(8,128)(2,1)}), bf16[3,8,256,128]{3,1,0,2:T(8,128)(2,1)}, u32[]{:S(2)}, u32[]{:S(2)}) %all-to-all-start.1) | async-done | bytes 1572896 | tf_op jit(solution)/shard_map/all_to_all | solution.py:131
  108.9 26.8 %all_to_all.144 = bf16[3,256,8,128]{3,2,0,1:T(8,128)(2,1)S(1)} all-to-all(bf16[3,256,8,128]{3,2,0,1:T(8,128)(2,1)} %copy.85), channel_id=1, replica_groups=mesh['row'=4,'col'=32] {'col'}, dimensions={1} | all-to-all | bytes 3145728 | tf_op jit(solution)/shard_map/all_to_all | solution.py:137
  141.7 4.5 %all-to-all-start.3 = ((bf16[3,8,256,128]{3,1,0,2:T(8,128)(2,1)}), bf16[3,8,256,128]{3,1,0,2:T(8,128)(2,1)}, u32[]{:S(2)}, u32[]{:S(2)}) async-start(bf16[3,8,256,128]{3,1,0,2:T(8,128)(2,1)} %copy.90), calls=%async_computation.3 | async-start | bytes 3145728 | tf_op jit(solution)/shard_map/all_to_all | solution.py:139
  149.7 18.1 %all-to-all-done.3 = bf16[3,8,256,128]{3,1,0,2:T(8,128)(2,1)} async-done(((bf16[3,8,256,128]{3,1,0,2:T(8,128)(2,1)}), bf16[3,8,256,128]{3,1,0,2:T(8,128)(2,1)}, u32[]{:S(2)}, u32[]{:S(2)}) %all-to-all-start.3) | async-done | bytes 1572896 | tf_op jit(solution)/shard_map/all_to_all | solution.py:139
  167.8 3.8 copy.92
  171.6 3.6 all_to_all.119
  175.2 4.6 %convolution_convert_fusion.1 = bf16[3,8,64,512]{3,2,1,0:T(8,128)(2,1)} fusion(bf16[512,512,1,1]{0,1,3,2:T(8,128)(2,1)} %bitcast.425, bf16[3,8,64,512]{3,2,1,0:T(8,128)(2,1)} %all_to_all.119, bf16[512,512,1,1]{1,0,3,2:T(8,128)(2,1)S(1)} %bitcast.420, bf16[8,64,512]{2,1,0:T(8,128)(2,1)} %convert_element_type.279), kind=kOutput, calls=%fused_computation.20 | convolution fusion | flops 1612972032 | bytes 4718592 | tf_op jit(solution)/shard_map/dot_general | solution.py:128
  179.8 5.0 %copy.94 = bf16[3,8,64,512]{2,1,0,3:T(8,128)(2,1)} copy(bf16[3,8,64,512]{3,2,1,0:T(8,128)(2,1)} %convolution_convert_fusion.1) | data formatting | bytes 3145728 | tf_op jit(solution)/shard_map/convert_element_type | solution.py:128
  184.8 5.0 %reshape.450 = bf16[4,2,98304]{2,1,0:T(2,128)(2,1)} reshape(bf16[512,3,8,64]{3,2,1,0:T(8,128)(2,1)} %bitcast.413) | data formatting | bytes 3145728
  189.8 26.0 %all_to_all.145 = bf16[4,2,98304]{2,1,0:T(2,128)(2,1)} all-to-all(bf16[4,2,98304]{2,1,0:T(2,128)(2,1)} %reshape.450), channel_id=1, replica_groups=mesh['row'=4,'col'=32] {'row'}, dimensions={0} | all-to-all | bytes 3145728 | tf_op jit(solution)/shard_map/all_to_all | solution.py:129
  215.8 4.9 %reshape.451 = bf16[512,3,8,64]{3,2,1,0:T(8,128)(2,1)} reshape(bf16[4,2,98304]{2,1,0:T(2,128)(2,1)} %all_to_all.145) | data formatting | bytes 3145728
  220.7 4.9 %copy.131 = bf16[3,8,64,4,128]{4,3,2,1,0:T(4,128)(2,1)} copy(bf16[3,8,64,4,128]{2,1,0,4,3:T(8,128)(2,1)} %bitcast.414) | data formatting | bytes 3145728 | tf_op jit(solution)/shard_map/all_to_all | solution.py:129
  235.4 27.5 %all_to_all.146 = bf16[3,8,256,128]{3,1,0,2:T(8,128)(2,1)S(1)} all-to-all(bf16[3,8,256,128]{3,1,0,2:T(8,128)(2,1)} %copy.99), channel_id=1, replica_groups=mesh['row'=4,'col'=32] {'col'}, dimensions={2} | all-to-all | bytes 3145728 | tf_op jit(solution)/shard_map/all_to_all | solution.py:131
  283.3 26.4 %all_to_all.147 = bf16[3,256,8,128]{3,2,0,1:T(8,128)(2,1)S(1)} all-to-all(bf16[3,256,8,128]{3,2,0,1:T(8,128)(2,1)} %copy.104), channel_id=1, replica_groups=mesh['row'=4,'col'=32] {'col'}, dimensions={1} | all-to-all | bytes 3145728 | tf_op jit(solution)/shard_map/all_to_all | solution.py:137
  315.6 4.5 %all-to-all-start.7 = ((bf16[3,8,256,128]{3,1,0,2:T(8,128)(2,1)}), bf16[3,8,256,128]{3,1,0,2:T(8,128)(2,1)}, u32[]{:S(2)}, u32[]{:S(2)}) async-start(bf16[3,8,256,128]{3,1,0,2:T(8,128)(2,1)} %copy.109), calls=%async_computation.7 | async-start | bytes 3145728 | tf_op jit(solution)/shard_map/all_to_all | solution.py:139
  323.5 18.0 %collective-permute-done = bf16[1,8,1,512]{3,2,1,0:T(2,128)(2,1)S(1)} collective-permute-done((bf16[1,8,1,512]{3,2,1,0:T(2,128)(2,1)S(1)}, bf16[1,8,1,512]{3,2,1,0:T(2,128)(2,1)S(1)}, u32[]{:S(2)}, u32[]{:S(2)}) %collective-permute-start) | collective-permute-done | bytes 8224 | tf_op jit(solution)/shard_map/ppermute | solution.py:28
  342.2 5.8 %collective-permute-start.3 = (bf16[1,1,66,512]{3,2,1,0:T(8,128)(2,1)S(1)}, bf16[1,1,66,512]{3,2,1,0:T(8,128)(2,1)S(1)}, u32[]{:S(2)}, u32[]{:S(2)}) collective-permute-start(bf16[1,1,66,512]{3,2,1,0:T(8,128)(2,1)S(1)} %get-tuple-element.47), channel_id=1, source_target_pairs={{1,0},{2,1},{3,2},{4,3},{5,4},{6,5},{7,6},{8,7},{9,8},{10,9},{11,1... | collective-permute-start | bytes 202760 | tf_op jit(solution)/shard_map/ppermute | solution.py:29
  353.8 3.8 copy.111
  357.6 3.6 all_to_all.135
  361.2 3.7 fusion.261
  367.0 3.2 collective-permute-start.5
  372.0 6.5 %collective-permute-start.7 = (bf16[1,1,66,512]{3,2,1,0:T(8,128)(2,1)S(1)}, bf16[1,1,66,512]{3,2,1,0:T(8,128)(2,1)S(1)}, u32[]{:S(2)}, u32[]{:S(2)}) collective-permute-start(bf16[1,1,66,512]{3,2,1,0:T(8,128)(2,1)S(1)} %get-tuple-element.45), channel_id=1, source_target_pairs={{1,0},{2,1},{3,2},{4,3},{5,4},{6,5},{7,6},{8,7},{9,8},{10,9},{11,1... | collective-permute-start | bytes 202760 | tf_op jit(solution)/shard_map/ppermute | solution.py:29
  389.1 6.2 %collective-permute-start.11 = (bf16[1,1,66,512]{3,2,1,0:T(8,128)(2,1)S(1)}, bf16[1,1,66,512]{3,2,1,0:T(8,128)(2,1)S(1)}, u32[]{:S(2)}, u32[]{:S(2)}) collective-permute-start(bf16[1,1,66,512]{3,2,1,0:T(8,128)(2,1)S(1)} %get-tuple-element.43), channel_id=1, source_target_pairs={{1,0},{2,1},{3,2},{4,3},{5,4},{6,5},{7,6},{8,7},{9,8},{10,9},{11,1... | collective-permute-start | bytes 202760 | tf_op jit(solution)/shard_map/ppermute | solution.py:29
  405.7 6.2 %collective-permute-start.15 = (bf16[1,1,66,512]{3,2,1,0:T(8,128)(2,1)S(1)}, bf16[1,1,66,512]{3,2,1,0:T(8,128)(2,1)S(1)}, u32[]{:S(2)}, u32[]{:S(2)}) collective-permute-start(bf16[1,1,66,512]{3,2,1,0:T(8,128)(2,1)S(1)} %get-tuple-element.41), channel_id=1, source_target_pairs={{1,0},{2,1},{3,2},{4,3},{5,4},{6,5},{7,6},{8,7},{9,8},{10,9},{11,1... | collective-permute-start | bytes 202760 | tf_op jit(solution)/shard_map/ppermute | solution.py:29
  422.5 6.2 %collective-permute-start.19 = (bf16[1,1,66,512]{3,2,1,0:T(8,128)(2,1)S(1)}, bf16[1,1,66,512]{3,2,1,0:T(8,128)(2,1)S(1)}, u32[]{:S(2)}, u32[]{:S(2)}) collective-permute-start(bf16[1,1,66,512]{3,2,1,0:T(8,128)(2,1)S(1)} %get-tuple-element.39), channel_id=1, source_target_pairs={{1,0},{2,1},{3,2},{4,3},{5,4},{6,5},{7,6},{8,7},{9,8},{10,9},{11,1... | collective-permute-start | bytes 202760 | tf_op jit(solution)/shard_map/ppermute | solution.py:29
  (191 shorter events, 134.4 us)
Async XLA Ops:
  0.6 3.4 copy-start
  13.4 26.1 %all-to-all-start = ((bf16[4,2,98304]{2,1,0:T(2,128)(2,1)}), bf16[4,2,98304]{2,1,0:T(2,128)(2,1)}, u32[]{:S(2)}, u32[]{:S(2)}) async-start(bf16[4,2,98304]{2,1,0:T(2,128)(2,1)} %reshape.448), calls=%async_computation | async-start | bytes 3145728 | tf_op jit(solution)/shard_map/all_to_all | solution.py:129
  54.5 33.9 %all-to-all-start.1 = ((bf16[3,8,256,128]{3,1,0,2:T(8,128)(2,1)}), bf16[3,8,256,128]{3,1,0,2:T(8,128)(2,1)}, u32[]{:S(2)}, u32[]{:S(2)}) async-start(bf16[3,8,256,128]{3,1,0,2:T(8,128)(2,1)} %copy.80), calls=%async_computation.1 | async-start | bytes 3145728 | tf_op jit(solution)/shard_map/all_to_all | solution.py:131
  66.8 33.3 %copy-start.3 = (f32[3,256,8,128]{1,3,2,0:T(8,128)}, f32[3,256,8,128]{1,3,2,0:T(8,128)S(1)}, u32[]{:S(2)}) copy-start(f32[3,256,8,128]{1,3,2,0:T(8,128)S(1)} %maximum_maximum_fusion) | copy-start | bytes 9437188
  94.3 3.0 copy-start.5
  141.7 4.5 %copy-start.2 = (s32[8,64,512]{2,1,0:T(8,128)S(1)}, s32[8,64,512]{2,1,0:T(8,128)}, u32[]{:S(2)}) copy-start(s32[8,64,512]{2,1,0:T(8,128)} %param.4) | copy-start | bytes 3145732
  141.7 26.1 %all-to-all-start.3 = ((bf16[3,8,256,128]{3,1,0,2:T(8,128)(2,1)}), bf16[3,8,256,128]{3,1,0,2:T(8,128)(2,1)}, u32[]{:S(2)}, u32[]{:S(2)}) async-start(bf16[3,8,256,128]{3,1,0,2:T(8,128)(2,1)} %copy.90), calls=%async_computation.3 | async-start | bytes 3145728 | tf_op jit(solution)/shard_map/all_to_all | solution.py:139
  315.6 4.5 %copy-start.23 = (bf16[8,64,512]{2,1,0:T(8,128)(2,1)S(1)}, bf16[8,64,512]{2,1,0:T(8,128)(2,1)}, u32[]{:S(2)}) copy-start(bf16[8,64,512]{2,1,0:T(8,128)(2,1)} %param.5) | copy-start | bytes 1572868
  315.6 38.3 %all-to-all-start.7 = ((bf16[3,8,256,128]{3,1,0,2:T(8,128)(2,1)}), bf16[3,8,256,128]{3,1,0,2:T(8,128)(2,1)}, u32[]{:S(2)}, u32[]{:S(2)}) async-start(bf16[3,8,256,128]{3,1,0,2:T(8,128)(2,1)} %copy.109), calls=%async_computation.7 | async-start | bytes 3145728 | tf_op jit(solution)/shard_map/all_to_all | solution.py:139
  320.1 21.4 %collective-permute-start = (bf16[1,8,1,512]{3,2,1,0:T(2,128)(2,1)S(1)}, bf16[1,8,1,512]{3,2,1,0:T(2,128)(2,1)S(1)}, u32[]{:S(2)}, u32[]{:S(2)}) collective-permute-start(bf16[1,8,1,512]{3,2,1,0:T(2,128)(2,1)S(1)} %get-tuple-element.66), channel_id=1, source_target_pairs={{0,32},{32,64},{64,96},{96,0},{1,33},{33,65},{65,97},{97,1},{2,34}... | collective-permute-start | bytes 24584 | tf_op jit(solution)/shard_map/ppermute | solution.py:28
  320.6 20.9 %collective-permute-start.1 = (bf16[1,8,1,512]{3,2,1,0:T(2,128)(2,1)S(1)}, bf16[1,8,1,512]{3,2,1,0:T(2,128)(2,1)S(1)}, u32[]{:S(2)}, u32[]{:S(2)}) collective-permute-start(bf16[1,8,1,512]{3,2,1,0:T(2,128)(2,1)S(1)} %get-tuple-element.67), channel_id=1, source_target_pairs={{32,0},{64,32},{96,64},{0,96},{33,1},{65,33},{97,65},{1,97},{34,2}... | collective-permute-start | bytes 24584 | tf_op jit(solution)/shard_map/ppermute | solution.py:29
  341.7 9.4 %collective-permute-start.2 = (bf16[1,1,66,512]{3,2,1,0:T(8,128)(2,1)S(1)}, bf16[1,1,66,512]{3,2,1,0:T(8,128)(2,1)S(1)}, u32[]{:S(2)}, u32[]{:S(2)}) collective-permute-start(bf16[1,1,66,512]{3,2,1,0:T(8,128)(2,1)S(1)} %get-tuple-element.46), channel_id=1, source_target_pairs={{0,1},{1,2},{2,3},{3,4},{4,5},{5,6},{6,7},{7,8},{8,9},{9,10},{10,1... | collective-permute-start | bytes 202760 | tf_op jit(solution)/shard_map/ppermute | solution.py:28
  342.2 8.8 %collective-permute-start.3 = (bf16[1,1,66,512]{3,2,1,0:T(8,128)(2,1)S(1)}, bf16[1,1,66,512]{3,2,1,0:T(8,128)(2,1)S(1)}, u32[]{:S(2)}, u32[]{:S(2)}) collective-permute-start(bf16[1,1,66,512]{3,2,1,0:T(8,128)(2,1)S(1)} %get-tuple-element.47), channel_id=1, source_target_pairs={{1,0},{2,1},{3,2},{4,3},{5,4},{6,5},{7,6},{8,7},{9,8},{10,9},{11,1... | collective-permute-start | bytes 202760 | tf_op jit(solution)/shard_map/ppermute | solution.py:29
  361.2 3.7 copy-start.20
  361.2 3.7 copy-start.21
  361.2 3.7 copy-start.22
  366.9 4.7 %collective-permute-start.4 = (bf16[1,8,1,512]{3,2,1,0:T(2,128)(2,1)S(1)}, bf16[1,8,1,512]{3,2,1,0:T(2,128)(2,1)S(1)}, u32[]{:S(2)}, u32[]{:S(2)}) collective-permute-start(bf16[1,8,1,512]{3,2,1,0:T(2,128)(2,1)S(1)} %get-tuple-element.64), channel_id=1, source_target_pairs={{0,32},{32,64},{64,96},{96,0},{1,33},{33,65},{65,97},{97,1},{2,34}... | collective-permute-start | bytes 24584 | tf_op jit(solution)/shard_map/ppermute | solution.py:28
  367.0 4.7 %collective-permute-start.5 = (bf16[1,8,1,512]{3,2,1,0:T(2,128)(2,1)S(1)}, bf16[1,8,1,512]{3,2,1,0:T(2,128)(2,1)S(1)}, u32[]{:S(2)}, u32[]{:S(2)}) collective-permute-start(bf16[1,8,1,512]{3,2,1,0:T(2,128)(2,1)S(1)} %get-tuple-element.65), channel_id=1, source_target_pairs={{32,0},{64,32},{96,64},{0,96},{33,1},{65,33},{97,65},{1,97},{34,2}... | collective-permute-start | bytes 24584 | tf_op jit(solution)/shard_map/ppermute | solution.py:29
  371.9 9.4 %collective-permute-start.6 = (bf16[1,1,66,512]{3,2,1,0:T(8,128)(2,1)S(1)}, bf16[1,1,66,512]{3,2,1,0:T(8,128)(2,1)S(1)}, u32[]{:S(2)}, u32[]{:S(2)}) collective-permute-start(bf16[1,1,66,512]{3,2,1,0:T(8,128)(2,1)S(1)} %get-tuple-element.44), channel_id=1, source_target_pairs={{0,1},{1,2},{2,3},{3,4},{4,5},{5,6},{6,7},{7,8},{8,9},{9,10},{10,1... | collective-permute-start | bytes 202760 | tf_op jit(solution)/shard_map/ppermute | solution.py:28
  372.0 9.4 %collective-permute-start.7 = (bf16[1,1,66,512]{3,2,1,0:T(8,128)(2,1)S(1)}, bf16[1,1,66,512]{3,2,1,0:T(8,128)(2,1)S(1)}, u32[]{:S(2)}, u32[]{:S(2)}) collective-permute-start(bf16[1,1,66,512]{3,2,1,0:T(8,128)(2,1)S(1)} %get-tuple-element.45), channel_id=1, source_target_pairs={{1,0},{2,1},{3,2},{4,3},{5,4},{6,5},{7,6},{8,7},{9,8},{10,9},{11,1... | collective-permute-start | bytes 202760 | tf_op jit(solution)/shard_map/ppermute | solution.py:29
  384.1 4.7 %collective-permute-start.8 = (bf16[1,8,1,512]{3,2,1,0:T(2,128)(2,1)S(1)}, bf16[1,8,1,512]{3,2,1,0:T(2,128)(2,1)S(1)}, u32[]{:S(2)}, u32[]{:S(2)}) collective-permute-start(bf16[1,8,1,512]{3,2,1,0:T(2,128)(2,1)S(1)} %get-tuple-element.62), channel_id=1, source_target_pairs={{0,32},{32,64},{64,96},{96,0},{1,33},{33,65},{65,97},{97,1},{2,34}... | collective-permute-start | bytes 24584 | tf_op jit(solution)/shard_map/ppermute | solution.py:28
  384.2 4.7 %collective-permute-start.9 = (bf16[1,8,1,512]{3,2,1,0:T(2,128)(2,1)S(1)}, bf16[1,8,1,512]{3,2,1,0:T(2,128)(2,1)S(1)}, u32[]{:S(2)}, u32[]{:S(2)}) collective-permute-start(bf16[1,8,1,512]{3,2,1,0:T(2,128)(2,1)S(1)} %get-tuple-element.63), channel_id=1, source_target_pairs={{32,0},{64,32},{96,64},{0,96},{33,1},{65,33},{97,65},{1,97},{34,2}... | collective-permute-start | bytes 24584 | tf_op jit(solution)/shard_map/ppermute | solution.py:29
  389.1 8.8 %collective-permute-start.10 = (bf16[1,1,66,512]{3,2,1,0:T(8,128)(2,1)S(1)}, bf16[1,1,66,512]{3,2,1,0:T(8,128)(2,1)S(1)}, u32[]{:S(2)}, u32[]{:S(2)}) collective-permute-start(bf16[1,1,66,512]{3,2,1,0:T(8,128)(2,1)S(1)} %get-tuple-element.42), channel_id=1, source_target_pairs={{0,1},{1,2},{2,3},{3,4},{4,5},{5,6},{6,7},{7,8},{8,9},{9,10},{10,1... | collective-permute-start | bytes 202760 | tf_op jit(solution)/shard_map/ppermute | solution.py:28
  389.1 8.8 %collective-permute-start.11 = (bf16[1,1,66,512]{3,2,1,0:T(8,128)(2,1)S(1)}, bf16[1,1,66,512]{3,2,1,0:T(8,128)(2,1)S(1)}, u32[]{:S(2)}, u32[]{:S(2)}) collective-permute-start(bf16[1,1,66,512]{3,2,1,0:T(8,128)(2,1)S(1)} %get-tuple-element.43), channel_id=1, source_target_pairs={{1,0},{2,1},{3,2},{4,3},{5,4},{6,5},{7,6},{8,7},{9,8},{10,9},{11,1... | collective-permute-start | bytes 202760 | tf_op jit(solution)/shard_map/ppermute | solution.py:29
  400.7 4.7 %collective-permute-start.12 = (bf16[1,8,1,512]{3,2,1,0:T(2,128)(2,1)S(1)}, bf16[1,8,1,512]{3,2,1,0:T(2,128)(2,1)S(1)}, u32[]{:S(2)}, u32[]{:S(2)}) collective-permute-start(bf16[1,8,1,512]{3,2,1,0:T(2,128)(2,1)S(1)} %get-tuple-element.60), channel_id=1, source_target_pairs={{0,32},{32,64},{64,96},{96,0},{1,33},{33,65},{65,97},{97,1},{2,34}... | collective-permute-start | bytes 24584 | tf_op jit(solution)/shard_map/ppermute | solution.py:28
  400.7 4.7 %collective-permute-start.13 = (bf16[1,8,1,512]{3,2,1,0:T(2,128)(2,1)S(1)}, bf16[1,8,1,512]{3,2,1,0:T(2,128)(2,1)S(1)}, u32[]{:S(2)}, u32[]{:S(2)}) collective-permute-start(bf16[1,8,1,512]{3,2,1,0:T(2,128)(2,1)S(1)} %get-tuple-element.61), channel_id=1, source_target_pairs={{32,0},{64,32},{96,64},{0,96},{33,1},{65,33},{97,65},{1,97},{34,2}... | collective-permute-start | bytes 24584 | tf_op jit(solution)/shard_map/ppermute | solution.py:29
  405.6 8.9 %collective-permute-start.14 = (bf16[1,1,66,512]{3,2,1,0:T(8,128)(2,1)S(1)}, bf16[1,1,66,512]{3,2,1,0:T(8,128)(2,1)S(1)}, u32[]{:S(2)}, u32[]{:S(2)}) collective-permute-start(bf16[1,1,66,512]{3,2,1,0:T(8,128)(2,1)S(1)} %get-tuple-element.40), channel_id=1, source_target_pairs={{0,1},{1,2},{2,3},{3,4},{4,5},{5,6},{6,7},{7,8},{8,9},{9,10},{10,1... | collective-permute-start | bytes 202760 | tf_op jit(solution)/shard_map/ppermute | solution.py:28
  405.7 8.8 %collective-permute-start.15 = (bf16[1,1,66,512]{3,2,1,0:T(8,128)(2,1)S(1)}, bf16[1,1,66,512]{3,2,1,0:T(8,128)(2,1)S(1)}, u32[]{:S(2)}, u32[]{:S(2)}) collective-permute-start(bf16[1,1,66,512]{3,2,1,0:T(8,128)(2,1)S(1)} %get-tuple-element.41), channel_id=1, source_target_pairs={{1,0},{2,1},{3,2},{4,3},{5,4},{6,5},{7,6},{8,7},{9,8},{10,9},{11,1... | collective-permute-start | bytes 202760 | tf_op jit(solution)/shard_map/ppermute | solution.py:29
  417.3 4.9 %collective-permute-start.16 = (bf16[1,8,1,512]{3,2,1,0:T(2,128)(2,1)S(1)}, bf16[1,8,1,512]{3,2,1,0:T(2,128)(2,1)S(1)}, u32[]{:S(2)}, u32[]{:S(2)}) collective-permute-start(bf16[1,8,1,512]{3,2,1,0:T(2,128)(2,1)S(1)} %get-tuple-element.58), channel_id=1, source_target_pairs={{0,32},{32,64},{64,96},{96,0},{1,33},{33,65},{65,97},{97,1},{2,34}... | collective-permute-start | bytes 24584 | tf_op jit(solution)/shard_map/ppermute | solution.py:28
  417.4 4.8 %collective-permute-start.17 = (bf16[1,8,1,512]{3,2,1,0:T(2,128)(2,1)S(1)}, bf16[1,8,1,512]{3,2,1,0:T(2,128)(2,1)S(1)}, u32[]{:S(2)}, u32[]{:S(2)}) collective-permute-start(bf16[1,8,1,512]{3,2,1,0:T(2,128)(2,1)S(1)} %get-tuple-element.59), channel_id=1, source_target_pairs={{32,0},{64,32},{96,64},{0,96},{33,1},{65,33},{97,65},{1,97},{34,2}... | collective-permute-start | bytes 24584 | tf_op jit(solution)/shard_map/ppermute | solution.py:29
  422.4 9.4 %collective-permute-start.18 = (bf16[1,1,66,512]{3,2,1,0:T(8,128)(2,1)S(1)}, bf16[1,1,66,512]{3,2,1,0:T(8,128)(2,1)S(1)}, u32[]{:S(2)}, u32[]{:S(2)}) collective-permute-start(bf16[1,1,66,512]{3,2,1,0:T(8,128)(2,1)S(1)} %get-tuple-element.38), channel_id=1, source_target_pairs={{0,1},{1,2},{2,3},{3,4},{4,5},{5,6},{6,7},{7,8},{8,9},{9,10},{10,1... | collective-permute-start | bytes 202760 | tf_op jit(solution)/shard_map/ppermute | solution.py:28
  422.5 9.3 %collective-permute-start.19 = (bf16[1,1,66,512]{3,2,1,0:T(8,128)(2,1)S(1)}, bf16[1,1,66,512]{3,2,1,0:T(8,128)(2,1)S(1)}, u32[]{:S(2)}, u32[]{:S(2)}) collective-permute-start(bf16[1,1,66,512]{3,2,1,0:T(8,128)(2,1)S(1)} %get-tuple-element.39), channel_id=1, source_target_pairs={{1,0},{2,1},{3,2},{4,3},{5,4},{6,5},{7,6},{8,7},{9,8},{10,9},{11,1... | collective-permute-start | bytes 202760 | tf_op jit(solution)/shard_map/ppermute | solution.py:29
  (17 other events, 25.7 us)
where the time goes:
time: 444 us; the launch traced here: 436 us
  blocking collectives  107 us (24%)
  waiting for transfers between devices  98.3 us (22%)
  local copies, waits for them, and re-layouts  87 us (20%)
  starting transfers between devices  71.3 us (16%)
  matrix products  38 us (9%)
  other arithmetic  32.5 us (7%)
    all_to_all x2, blocking collectives, backward(): lax.all_to_all(spread, 'col', split_axis=1, concat_axis=2, tiled=True)  53.2 us
    ppermute x10, starting transfers between devices, extended(): after = lax.ppermute(initial, axis, down)  46.7 us
    ppermute x10, waiting for transfers between devices, extended(): before = lax.ppermute(last, axis, up)  37.9 us
    all_to_all x1, blocking collectives, forward(): lax.all_to_all(spread, 'col', split_axis=2, concat_axis=1, tiled=True)  27.5 us
    all_to_all x1, blocking collectives, forward(): lax.all_to_all(spread, 'row', split_axis=3, concat_axis=2, tiled=True)  26 us
    unnamed x54, local copies, waits for them, and re-layouts  23.1 us
    all_to_all x1, waiting for transfers between devices, forward(): lax.all_to_all(spread, 'row', split_axis=3, concat_axis=2, tiled=True)  21.6 us
    all_to_all x1, waiting for transfers between devices, forward(): lax.all_to_all(spread, 'col', split_axis=2, concat_axis=1, tiled=True)  20.5 us
  transfers between devices with their start and end apart: 24, of which 13 were waited for; matrix products, arithmetic and copies ran while one was open for 2% of the time, Pallas kernels for 0%

commit v1 on v0

v1 whole, which is shorter than its diff:
```python
import numpy as np
import jax
import jax.numpy as jnp
import ml_dtypes
from jax import lax
from jax.experimental import pallas as pl
from jax.experimental.pallas import tpu as pltpu
from jax.sharding import PartitionSpec as P

SECTIONS = 5
MESH = pl.DeviceIdType.MESH
BF = jnp.bfloat16
F32 = jnp.float32
TWO_PI = 2.0 * np.pi
PLANE_ORDER = (
    (1, 0), (3, 0), (0, 1), (0, 3), (1, 1), (3, 3), (1, 3), (3, 1),
    (2, 0), (0, 2), (2, 1), (1, 2), (2, 3), (3, 2), (2, 2),
)


def numpy_tables():
    def half(values):
        return values.astype(np.float32).astype(ml_dtypes.bfloat16)

    x = np.arange(512)
    h, ri, d, k = np.meshgrid(np.arange(2), np.arange(2), np.arange(8), np.arange(16), indexing="ij")
    m = (d * 32 + h * 16 + k).reshape(-1)
    ri = ri.reshape(-1)
    angle = (np.outer(x, m) % 512) * (TWO_PI / 512)
    fx = np.where(ri == 0, np.cos(angle), -np.sin(angle)) / np.sqrt(512.0)
    bx = (fx * np.where(m == 0, 1.0, 2.0)).T
    y = np.arange(256)
    angle = (np.outer(y, y) % 256) * (TWO_PI / 256)
    c, s = np.cos(angle) / 16.0, np.sin(angle) / 16.0
    real = np.concatenate([c, s], 1).reshape(16, 1, 16, 512)
    imag = np.concatenate([-s, c], 1).reshape(16, 1, 16, 512)
    ty = np.concatenate([real, imag], 1).reshape(512, 512)
    n = np.arange(16)
    angle = (np.outer(n, n) % 16) * (TWO_PI / 16)
    c, s = np.cos(angle) / 4.0, np.sin(angle) / 4.0
    cs = np.zeros((8, 256, 512))
    csi = np.zeros((8, 256, 512))
    tw = np.zeros((8, 2, 16, 256))
    k = np.arange(16)
    for d in range(8):
        for low in range(2):
            for p in range(8):
                zp = low * 8 + (p - d) % 8
                at = low * 128 + p * 16
                for k2 in range(16):
                    cs[d, at + k, k2 * 16 + k] = c[zp, k2]
                    cs[d, at + k, 256 + k2 * 16 + k] = s[zp, k2]
                    csi[d, k2 * 16 + k, at + k] = c[zp, k2]
                    csi[d, k2 * 16 + k, 256 + at + k] = s[zp, k2]
                tw[d, 0, :, at : at + 16] = np.cos(TWO_PI * zp * n / 256)[:, None] / 4.0
                tw[d, 1, :, at : at + 16] = np.sin(TWO_PI * zp * n / 256)[:, None] / 4.0
    return dict(
        fx=half(fx), bx=half(bx), ty=half(ty), tyi=half(ty.T), cs=half(cs), csi=half(csi),
        tw=tw.astype(np.float32),
    )


TABLES = ("fx", "ty", "tw", "cs", "csi", "tyi", "bx")
ROTATED = ("cs", "tw", "csi")


def radix4(a, sign):
    def add(u, v):
        return u[0] + v[0], u[1] + v[1]

    def sub(u, v):
        return u[0] - v[0], u[1] - v[1]

    t0, t1 = add(a[0], a[2]), sub(a[0], a[2])
    t2, t3 = add(a[1], a[3]), sub(a[1], a[3])
    t3 = (t3[1], -t3[0]) if sign > 0 else (-t3[1], t3[0])
    return add(t0, t2), add(t1, t3), sub(t0, t2), sub(t1, t3)


def turned_by(value, j, sign):
    if j == 0:
        return value
    c, s = float(np.cos(TWO_PI * j / 16)), float(np.sin(TWO_PI * j / 16)) * sign
    re, im = value
    return re * c + im * s, im * c - re * s


def merge(tiles, place):
    for bit in (1, 2, 4):
        take = (place & bit) != 0
        tiles = [jnp.where(take, tiles[(m + bit) % 8], tiles[m]) for m in range(8)]
    return tiles


def dot(a, b):
    return jnp.dot(a, b, preferred_element_type=F32)


def mixer_kernel(*refs):
    force_h, mask_h, scalar_h = refs[:3]
    count = len(TABLES)
    tables_h = dict(zip(TABLES, refs[3 : 3 + count]))
    velocity_h, conc_h = refs[3 + count : 5 + count]
    (field, mask, scalar, *rest) = refs[5 + count :]
    tab = dict(zip(TABLES, rest[:count]))
    (gain, inv, sa, ra, sb, rb, sbi, rbi, sai, rai, spec, first, second, lines, big, mid,
     zsend, zrecv, ysend, yrecv, coef, state, conc,
     in_sem, tab_sem, a_send, a_recv, b_send, b_recv, z_ssem, z_rsem, y_ssem, y_rsem, out_sem) = rest[count:]

    r = lax.axis_index("row")
    col = lax.axis_index("col")
    e = col // 2
    xl = col % 2
    d = xl * 4 + r

    def load(source, target, sem):
        copy = pltpu.make_async_copy(source, target, sem)
        copy.start()
        return copy

    def load_table(name):
        source = tables_h[name]
        sem = tab_sem.at[TABLES.index(name)]
        return load(source.at[d] if name in ROTATED else source, tab[name], sem)

    loads = {0: load(force_h.at[0], field.at[0], in_sem.at[0]), "fx": load_table("fx")}
    for i in (1, 2):
        loads[i] = load(force_h.at[i], field.at[i], in_sem.at[i])
    loads["scalar"] = load(scalar_h, scalar, in_sem.at[4])
    for name in TABLES[1:]:
        loads[name] = load_table(name)
    loads["mask"] = load(mask_h, mask, in_sem.at[3])

    core = r & 1
    x = (r // 2) * 2 + xl
    y_at, z_at = e // 4, e & 3

    def x_peer(step, of_core):
        at = (x + step * (1 + 2 * core)) & 3
        low = at & 1
        row = (at - low) + of_core
        return low * 4 + row, (row, e * 2 + low)

    def plane_peer(dy, dz):
        to = ((y_at + dy + core * (3 * dz - dy)) & 3) * 4 + ((z_at + dz + core * (3 * dy - dz)) & 3)
        return to, (r, to * 2 + xl)

    x_peers = [
        x_peer(step, core if same else 1 - core)
        for step, same in ((1, 1), (3, 1), (1, 0), (3, 0), (2, 1), (2, 0), (0, 0))
    ]
    plane_peers = [plane_peer(dy, dz) for dy, dz in PLANE_ORDER]

    z_up = (r, lax.rem(col + 1, 32))
    z_down = (r, lax.rem(col + 31, 32))
    y_up = (lax.rem(r + 1, 4), col)
    y_down = (lax.rem(r + 3, 4), col)

    barrier = pltpu.get_barrier_semaphore()

    for _, device in x_peers + plane_peers:
        pl.semaphore_signal(barrier, inc=1, device_id=device, device_id_type=MESH)
    across = (r, lax.rem(col + 31 + 2 * xl, 32))
    pl.semaphore_signal(barrier, inc=1, device_id=across, device_id_type=MESH)
    pl.semaphore_wait(barrier, 23)

    def remote(source, target, ssem, rsem, device):
        return pltpu.make_async_remote_copy(
            src_ref=source, dst_ref=target, send_sem=ssem, recv_sem=rsem,
            device_id=device, device_id_type=MESH)

    my_rows = pl.ds(pl.multiple_of(r * 64, 64), 64)
    my_lanes = pl.ds(pl.multiple_of(xl * 128, 128), 128)
    my_slab = pl.ds(pl.multiple_of(e * 32, 32), 32)

    def send_a(t, i):
        target = ra.at[t, i, :, my_rows, my_lanes]
        recv = a_recv.at[2 * t, i]

        for to, device in x_peers:
            remote(sa.at[i, to], target, a_send.at[2 * t, i], recv, device).start()
        pltpu.make_async_copy(sa.at[i, d], target, recv).start()

    def send_ai(t, i):
        target = rai.at[t, i, d]
        recv = a_recv.at[2 * t + 1, i]

        def piece(to):
            rows = pl.ds(pl.multiple_of((to & 3) * 64, 64), 64)
            lanes = pl.ds(pl.multiple_of((to // 4) * 128, 128), 128)
            return sai.at[i, :, rows, lanes]

        for to, device in x_peers:
            remote(piece(to), target, a_send.at[2 * t + 1, i], recv, device).start()
        pltpu.make_async_copy(piece(d), target, recv).start()

    def send_b(source, into, k, t, i):
        target = into.at[t, i, my_slab]
        recv = b_recv.at[k, i]

        for to, device in plane_peers:
            slab = source.at[i, pl.ds(pl.multiple_of(to * 32, 32), 32)]
            remote(slab, target, b_send.at[k, i], recv, device).start()
        pltpu.make_async_copy(source.at[i, my_slab], target, recv).start()

    def arrived(buffer, sem):
        pltpu.make_async_copy(buffer, buffer, sem).wait()

    def sent_a(k, i):
        part = sa.at[i, pl.ds(0, 7)]
        pltpu.make_async_copy(part, part, a_send.at[k, i]).wait()

    def sent_b(k, i):
        part = sb.at[i, pl.ds(0, 480)]
        pltpu.make_async_copy(part, part, b_send.at[k, i]).wait()

    def send_z(s, q):
        rows = pl.ds(16 * q, 16)
        for side, device in ((0, z_down), (1, z_up)):
            remote(zsend.at[s, side, rows], zrecv.at[s, 1 - side, rows],
                   z_ssem.at[s, side], z_rsem.at[s, 1 - side, q], device).start()

    def send_y(s, side):
        remote(ysend.at[s, side], yrecv.at[s, 1 - side], y_ssem.at[s, side], y_rsem.at[s, 1 - side],
               (y_down, y_up)[side]).start()

    place = lax.broadcasted_iota(jnp.int32, (64, 128), 1) // 16

    def x_forward(t, c):
        spread = dot(field[c].reshape(512, 512), tab["fx"][...])
        for j in range(4):
            tiles = []
            for z in range(8):
                tile = spread[z * 64 : z * 64 + 64, j * 128 : j * 128 + 128]
                tiles.append(pltpu.roll(tile, 16 * z, 1) if z else tile)
            tiles = merge(tiles, place)
            for to in range(8):
                sa[3 * (j // 2) + c, to, j % 2] = tiles[-to % 8].astype(BF)
        send_a(t, c)

    def x_inverse(t, c):
        for j in range(4):
            tiles = [rai[t, 3 * (j // 2) + c, source, j % 2].astype(F32) for source in range(8)]
            tiles = merge(tiles, place)
            for z in range(8):
                tile = tiles[-z % 8]
                tile = pltpu.roll(tile, 128 - 16 * z, 1) if z else tile
                lines[z * 64 : z * 64 + 64, j * 128 : j * 128 + 128] = tile.astype(BF)
        values = dot(lines[...], tab["bx"][...]).astype(BF).reshape(8, 64, 512)
        if t == 0:
            values = (values.astype(F32) * mask[...].astype(F32)).astype(BF)
        field[c] = values

    def y_forward(t, i):
        arrived(ra.at[t, i], a_recv.at[2 * t, i])
        sb[i] = dot(tab["ty"][...], ra[t, i].reshape(512, 256)).astype(BF)
        send_b(sb, rb, 2 * t, t, i)

    def y_inverse(t, i):
        arrived(rbi.at[t, i], b_recv.at[2 * t + 1, i])
        sai[i] = dot(tab["tyi"][...], rbi[t, i]).astype(BF).reshape(2, 256, 256)
        send_ai(t, i)

    def z_forward(t, i):
        arrived(rb.at[t, i], b_recv.at[2 * t, i])
        for half in range(2):
            lanes = slice(half * 128, half * 128 + 128)

            def source(e_from, ri):
                return rb[t, i, e_from * 32 + ri * 16 : e_from * 32 + ri * 16 + 16, lanes].astype(F32)

            for low in range(4):
                out = radix4([(source(low + 4 * j, 0), source(low + 4 * j, 1)) for j in range(4)], 1)
                for k, value in enumerate(out):
                    mid[low, k, 0, :, lanes], mid[low, k, 1, :, lanes] = turned_by(value, low * k, 1)
            for k in range(4):
                out = radix4([(mid[low, k, 0, :, lanes], mid[low, k, 1, :, lanes]) for low in range(4)], 1)
                for high, (re, im) in enumerate(out):
                    k1 = k + 4 * high
                    wc, ws = tab["tw"][0, k1 : k1 + 1, lanes], tab["tw"][1, k1 : k1 + 1, lanes]
                    big[k1 * 16 : k1 * 16 + 16, lanes] = (re * wc + im * ws).astype(BF)
                    big[256 + k1 * 16 : 256 + k1 * 16 + 16, lanes] = (im * wc - re * ws).astype(BF)
        both = dot(big[...], tab["cs"][...])
        spec[i, 0] = both[:256, :256] + both[256:, 256:]
        spec[i, 1] = both[256:, :256] - both[:256, 256:]

    def z_inverse(source, t, i):
        both = dot(source[i].reshape(512, 256), tab["csi"][...])
        for half in range(2):
            lanes = slice(half * 128, half * 128 + 128)
            other = slice(256 + half * 128, 256 + half * 128 + 128)

            def value(k1):
                upper, lower = slice(k1 * 16, k1 * 16 + 16), slice(256 + k1 * 16, 256 + k1 * 16 + 16)
                re = both[upper, lanes] - both[lower, other]
                im = both[lower, lanes] + both[upper, other]
                wc, ws = tab["tw"][0, k1 : k1 + 1, lanes], tab["tw"][1, k1 : k1 + 1, lanes]
                return re * wc - im * ws, im * wc + re * ws

            for low in range(4):
                out = radix4([value(low + 4 * j) for j in range(4)], -1)
                for k, turned in enumerate(out):
                    mid[low, k, 0, :, lanes], mid[low, k, 1, :, lanes] = turned_by(turned, low * k, -1)
            for k in range(4):
                out = radix4([(mid[low, k, 0, :, lanes], mid[low, k, 1, :, lanes]) for low in range(4)], -1)
                for high, (re, im) in enumerate(out):
                    to = (k + 4 * high) * 32
                    sbi[i, to : to + 16, lanes] = re.astype(BF)
                    sbi[i, to + 16 : to + 32, lanes] = im.astype(BF)
        send_b(sbi, rbi, 2 * t + 1, t, i)

    lane = lax.broadcasted_iota(jnp.int32, (16, 256), 1)
    unit_long, unit = np.float32(TWO_PI / 512), np.float32(TWO_PI / 256)
    index_y = e * 16 + lax.broadcasted_iota(jnp.int32, (16, 256), 0)
    wave_y = jnp.where(index_y < 128, index_y, index_y - 256).astype(F32) * unit

    def along_x(h):
        return (d * 32 + h * 16 + (lane & 15)).astype(F32) * unit_long

    def along_z(k1):
        index_z = k1 + 16 * (lane // 16)
        return index_z, jnp.where(index_z < 128, index_z, index_z - 256).astype(F32) * unit

    def factors(step, _):
        h, k1 = step // 16, step & 15
        wave_x = along_x(h)
        index_z, wave_z = along_z(k1)
        ksq = wave_x * wave_x + wave_y * wave_y + wave_z * wave_z
        edge = (index_y == 128) | (index_z == 128)
        rows = pl.ds(pl.multiple_of(k1 * 16, 16), 16)
        gain[h, rows] = jnp.where(edge, 0.0, 1.0 / (0.05 * ksq + 0.5))
        inv[h, rows] = jnp.where(ksq > 0.0, 1.0 / jnp.where(ksq > 0.0, ksq, 1.0), 0.0)
        return _

    def project(t, h):
        wave_x = along_x(h)

        def one(k1, _):
            wave_z = along_z(k1)[1]
            rows = pl.ds(pl.multiple_of(k1 * 16, 16), 16)
            g, n = gain[h, rows], inv[h, rows]
            for ri in range(2):
                w = [spec[3 * h + c, ri, rows] for c in range(3)]
                along = (wave_x * w[0] + wave_y * w[1] + wave_z * w[2]) * n
                for c, wave in enumerate((wave_x, wave_y, wave_z)):
                    value = g * (w[c] - wave * along)
                    if t == 0:
                        first[3 * h + c, ri, rows] = value.astype(BF)
                    else:
                        second[3 * h + c, ri, rows] = (first[3 * h + c, ri, rows].astype(F32) - value).astype(BF)
            return _

        lax.fori_loop(0, 16, one, 0)

    def each(count, step):
        def body(i, _):
            step(i)
            return _

        lax.fori_loop(0, count, body, 0)

    def spectral(t, source):
        def step(n):
            @pl.when(n < 6)
            def _():
                y_forward(t, n)

            @pl.when(((n >= 1) & (n <= 3)) | ((n >= 6) & (n <= 8)))
            def _():
                z_forward(t, jnp.where(n <= 3, n - 1, n - 3))

            @pl.when((n == 3) | (n == 8))
            def _():
                project(t, jnp.where(n == 3, 0, 1))

            @pl.when((n == 3) | (n == 5) | (n == 6) | ((n >= 8) & (n <= 10)))
            def _():
                z_inverse(source, t, jnp.where(n == 3, 0, jnp.where(n <= 6, n - 4, n - 5)))

            @pl.when((n == 5) | (n >= 8))
            def _():
                y_inverse(t, jnp.where(n == 5, 0, n - 7))

        each(13, step)

    loads["fx"].wait()
    for i in range(3):
        loads[i].wait()
    each(3, lambda c: x_forward(0, c))
    each(3, lambda c: send_a(0, c + 3))
    lax.fori_loop(0, 32, factors, 0)
    loads["scalar"].wait()
    for z in range(8):
        state[0, z + 1, pl.ds(8, 64), :] = scalar[z].astype(F32)
        ysend[0, 0, pl.ds(z, 1), :] = state[0, z + 1, pl.ds(8, 1), :]
        ysend[0, 1, pl.ds(z, 1), :] = state[0, z + 1, pl.ds(71, 1), :]
    zsend[0, 0] = scalar[0]
    zsend[0, 1] = scalar[7]
    for q in range(4):
        send_z(0, q)
    for side in range(2):
        send_y(0, side)
    for name in TABLES[1:]:
        loads[name].wait()
    loads["mask"].wait()
    spectral(0, first)

    def back_in_x(t, c):
        for i in (c, c + 3):
            arrived(rai.at[t, i], a_recv.at[2 * t + 1, i])
        x_inverse(t, c)

    def sent(t, c):
        for i in (c, c + 3):
            sent_b(2 * t, i)
            sent_b(2 * t + 1, i)
            sent_a(2 * t + 1, i)

    def middle(c):
        back_in_x(0, c)
        for i in (c, c + 3):
            sent_a(0, i)
        x_forward(1, c)
        sent(0, c)

    each(3, middle)
    each(3, lambda c: send_a(1, c + 3))
    spectral(1, second)

    def coefficients(z, c):
        fluid = 0.25 * (1.0 - mask[z].astype(F32))
        u = field[c, z].astype(F32)
        below = fluid * (0.25 + jnp.maximum(u, 0.0))
        above = fluid * (0.25 - jnp.minimum(u, 0.0))
        coef[2 * c, z] = below
        coef[2 * c + 1, z] = above
        start = jnp.where(c == 0, jnp.ones_like(u), coef[6, z])
        coef[6, z] = start - (below + above)
        return c

    def last(c):
        back_in_x(1, c)
        pltpu.make_async_copy(field.at[c], velocity_h.at[c], out_sem.at[c]).start()
        lax.fori_loop(0, 8, coefficients, c)
        for i in (c, c + 3):
            sent_a(2, i)
        sent(1, c)

    each(3, last)

    def section(s, carry):
        now, later = s & 1, (s + 1) & 1

        def block(z, q, below_z, above_z):
            at = 8 + 16 * q
            rows, cells = pl.ds(at, 16), pl.ds(16 * q, 16)
            center = state[now, z, rows]
            new = coef[6, z - 1, cells] * center
            new = new + coef[0, z - 1, cells] * pltpu.roll(center, 1, 1)
            new = new + coef[1, z - 1, cells] * pltpu.roll(center, 511, 1)
            new = new + coef[2, z - 1, cells] * state[now, z, pl.ds(at - 1, 16)]
            new = new + coef[3, z - 1, cells] * state[now, z, pl.ds(at + 1, 16)]
            new = new + coef[4, z - 1, cells] * below_z + coef[5, z - 1, cells] * above_z
            state[later, z, rows] = new
            return new

        for q in (1, 2, 0, 3):
            rows, cells = pl.ds(8 + 16 * q, 16), pl.ds(16 * q, 16)
            if q in (0, 3):
                side = q // 3
                arrived(yrecv.at[s, side], y_rsem.at[s, side])
                for z in range(8):
                    state[now, z + 1, pl.ds(7 + 65 * side, 1), :] = yrecv[s, side, pl.ds(z, 1), :]
            for side in range(2):
                arrived(zrecv.at[s, side, cells], z_rsem.at[s, side, q])
            bottom = block(1, q, zrecv[s, 0, cells].astype(F32), state[now, 2, rows])
            top = block(8, q, state[now, 7, rows], zrecv[s, 1, cells].astype(F32))

            @pl.when(s < SECTIONS - 1)
            def _():
                zsend[s + 1, 0, cells] = bottom.astype(BF)
                zsend[s + 1, 1, cells] = top.astype(BF)
                send_z(s + 1, q)

            def inner(z, _):
                block(z, q, state[now, z - 1, rows], state[now, z + 1, rows])
                return _

            lax.fori_loop(2, 8, inner, 0)
            if q in (0, 3):
                side = q // 3

                @pl.when(s < SECTIONS - 1)
                def _():
                    for z in range(8):
                        ysend[s + 1, side, pl.ds(z, 1), :] = state[later, z + 1, pl.ds(8 + 63 * side, 1), :]
                    send_y(s + 1, side)
        return carry

    lax.fori_loop(0, SECTIONS, section, 0)
    for z in range(8):
        conc[z] = state[SECTIONS % 2, z + 1, pl.ds(8, 64), :].astype(BF)

    for s in range(SECTIONS):
        for i in range(2):
            arrived(zsend.at[s, i], z_ssem.at[s, i])
            arrived(ysend.at[s, i], y_ssem.at[s, i])
    out = pltpu.make_async_copy(conc, conc_h, out_sem.at[3])
    out.start()
    for c in range(3):
        pltpu.make_async_copy(field.at[c], velocity_h.at[c], out_sem.at[c]).wait()
    out.wait()


def local(force, mask, scalar):
    tables = numpy_tables()
    vm = pltpu.VMEM
    dma = pltpu.SemaphoreType.DMA
    scratch = [vm((3, 8, 64, 512), BF), vm((8, 64, 512), jnp.int32), vm((8, 64, 512), BF)]
    for name in TABLES:
        value = tables[name]
        shape = value.shape[1:] if name in ROTATED else value.shape
        scratch.append(vm(shape, value.dtype))
    scratch += [
        vm((2, 256, 256), F32), vm((2, 256, 256), F32),
        vm((6, 8, 2, 64, 128), BF), vm((2, 6, 2, 256, 256), BF),
        vm((6, 512, 256), BF), vm((2, 6, 512, 256), BF),
        vm((6, 512, 256), BF), vm((2, 6, 512, 256), BF),
        vm((6, 2, 256, 256), BF), vm((2, 6, 8, 2, 64, 128), BF),
        vm((6, 2, 256, 256), F32), vm((6, 2, 256, 256), BF), vm((6, 2, 256, 256), BF),
        vm((512, 512), BF), vm((512, 256), BF), vm((4, 4, 2, 16, 256), F32),
        vm((SECTIONS, 2, 64, 512), BF), vm((SECTIONS, 2, 64, 512), BF),
        vm((SECTIONS, 2, 8, 512), F32), vm((SECTIONS, 2, 8, 512), F32),
        vm((7, 8, 64, 512), F32), vm((2, 10, 80, 512), F32), vm((8, 64, 512), BF),
        dma((5,)), dma((len(TABLES),)),
        dma((4, 6)), dma((4, 6)), dma((4, 6)), dma((4, 6)),
        dma((SECTIONS, 2)), dma((SECTIONS, 2, 4)), dma((SECTIONS, 2)), dma((SECTIONS, 2)),
        dma((4,)),
    ]
    any_spec = pl.BlockSpec(memory_space=pl.ANY)
    velocity, conc = pl.pallas_call(
        mixer_kernel,
        out_shape=(
            jax.ShapeDtypeStruct((3, 8, 64, 512), BF),
            jax.ShapeDtypeStruct((8, 64, 512), BF),
        ),
        in_specs=[any_spec] * (3 + len(TABLES)),
        out_specs=(any_spec, any_spec),
        scratch_shapes=scratch,
        compiler_params=pltpu.CompilerParams(
            collective_id=0, has_side_effects=True, vmem_limit_bytes=62 * 1024 * 1024
        ),
        name="mixer",
    )(
        force,
        mask,
        scalar,
        *[jnp.asarray(tables[name]) for name in TABLES],
    )
    return velocity, conc


def solution(mesh):
    placed = (P(None, "col", "row", None), P("col", "row", None), P("col", "row", None))
    return jax.shard_map(
        local,
        mesh=mesh,
        in_specs=placed,
        out_specs=(P(None, "col", "row", None), P("col", "row", None)),
        check_vma=False,
    )
```

time: 444 us -> 146 us (0.33); the launches traced: 436 us -> 146 us
  Pallas kernels: 0 us -> 142 us
  blocking collectives: 107 us -> 0 us
  waiting for transfers between devices: 98.3 us -> 0 us
  local copies, waits for them, and re-layouts: 87 us -> 3.56 us
  starting transfers between devices: 71.3 us -> 0 us
  matrix products: 38 us -> 0 us
  other arithmetic: 32.5 us -> 0 us
    pallas_call x0 -> x1, Pallas kernels: none -> 142 us  [local(): pl.pallas_call(mixer_kernel, out_shape=(jax.ShapeDtypeStruct((3, 8, 64, 5...]
    all_to_all x4 -> x0, blocking collectives: 107 us -> none  [the longest x2 53.2 us: backward(): lax.all_to_all(spread, 'col', split_axis=1, concat_axis=2, tiled=True)]
    all_to_all x4 -> x0, waiting for transfers between devices: 60.3 us -> none  [the longest x1 21.6 us: forward(): lax.all_to_all(spread, 'row', split_axis=3, concat_axis=2, tiled=True)]
    ppermute x20 -> x0, starting transfers between devices: 48.4 us -> none  [the longest x10 46.7 us: extended(): after = lax.ppermute(initial, axis, down)]
    ppermute x20 -> x0, waiting for transfers between devices: 38 us -> none  [the longest x10 37.9 us: extended(): before = lax.ppermute(last, axis, up)]
    dot_general x19 -> x0, matrix products: 38 us -> none  [the longest x8 15.3 us: pair_pass(): jnp.einsum(pattern, sine, spectra, preferred_element_type=jnp.float32)]
    all_to_all x12 -> x0, local copies, waits for them, and re-layouts: 37.3 us -> none  [the longest x4 14.8 us: backward(): lax.all_to_all(spread, 'row', split_axis=2, concat_axis=3, tiled=True)]
    all_to_all x4 -> x0, starting transfers between devices: 22.9 us -> none  [the longest x1 9.57 us: forward(): lax.all_to_all(spread, 'col', split_axis=2, concat_axis=1, tiled=True)]
  transfers between devices with their start and end apart: 24 -> 0, of which waited for: 13 -> 0; matrix products, arithmetic and copies ran while one was open for 2% -> 0% of each run, Pallas kernels for 0% -> 0%
where the time goes in v1:
time: 146 us
  Pallas kernels  142 us (97%)
  local copies, waits for them, and re-layouts  3.56 us (2%)
    pallas_call x1, Pallas kernels, local(): pl.pallas_call(mixer_kernel, out_shape=(jax.ShapeDtypeStruct((3, 8, 64, 5...  142 us
    unnamed x4, local copies, waits for them, and re-layouts  3.56 us

profile of v1, /device:TPU:0, one launch (start us, length us, event | category | flops | bytes accessed | tf_op | source)
XLA Modules:
  0.0 146.1 jit_solution(13802329111559920814)
XLA Ops:
  0.6 141.9 %mixer.1 = (bf16[3,8,64,512]{3,2,1,0:T(8,128)(2,1)}, bf16[8,64,512]{2,1,0:T(8,128)(2,1)}) custom-call(bf16[3,8,64,512]{3,2,1,0:T(8,128)(2,1)} %refs_0_.1, s32[8,64,512]{2,1,0:T(8,128)} %refs_1_.1, bf16[8,64,512]{2,1,0:T(8,128)(2,1)} %refs_2_.1, bf16[512,512]{1,0:T(8,128)(2,1)} %constant.14.clone.refs_3_, bf16[512,512]{1,0:T(8,128)(2,1)} %constant.15.clone.refs_4_, ...), custom_call_target="tpu_custom_call" | custom-call | tf_op jit(solution)/shard_map/mixer/pallas_call | solution.py:541
  142.5 0.0 copy-start
  142.6 2.8 %copy.14 = bf16[3,8,64,512]{3,2,1,0:T(8,128)(2,1)} copy(bf16[3,8,64,512]{3,2,1,0:T(8,128)(2,1)} %get-tuple-element.4) | data formatting | bytes 3145728
  145.3 0.0 copy-done
  145.3 0.8 copy.15
Async XLA Ops:
  142.5 2.8 %copy-start = (bf16[8,64,512]{2,1,0:T(8,128)(2,1)S(1)}, bf16[8,64,512]{2,1,0:T(8,128)(2,1)}, u32[]{:S(2)}) copy-start(bf16[8,64,512]{2,1,0:T(8,128)(2,1)} %get-tuple-element.5) | copy-start | bytes 1572868

commit v2 on v1

--- a/solution.py
+++ b/solution.py
@@ -226,17 +226,17 @@
 
     place = lax.broadcasted_iota(jnp.int32, (64, 128), 1) // 16
 
-    def x_forward(t, c):
-        spread = dot(field[c].reshape(512, 512), tab["fx"][...])
-        for j in range(4):
+    def x_forward(t, c, h):
+        spread = dot(field[c].reshape(512, 512), tab["fx"][:, h * 256 : h * 256 + 256])
+        for ri in range(2):
             tiles = []
             for z in range(8):
-                tile = spread[z * 64 : z * 64 + 64, j * 128 : j * 128 + 128]
+                tile = spread[z * 64 : z * 64 + 64, ri * 128 : ri * 128 + 128]
                 tiles.append(pltpu.roll(tile, 16 * z, 1) if z else tile)
             tiles = merge(tiles, place)
             for to in range(8):
-                sa[3 * (j // 2) + c, to, j % 2] = tiles[-to % 8].astype(BF)
-        send_a(t, c)
+                sa[3 * h + c, to, ri] = tiles[-to % 8].astype(BF)
+        send_a(t, 3 * h + c)
 
     def x_inverse(t, c):
         for j in range(4):
@@ -386,8 +386,8 @@
     loads["fx"].wait()
     for i in range(3):
         loads[i].wait()
-    each(3, lambda c: x_forward(0, c))
-    each(3, lambda c: send_a(0, c + 3))
+    each(3, lambda c: x_forward(0, c, 0))
+    each(3, lambda c: x_forward(0, c, 1))
     lax.fori_loop(0, 32, factors, 0)
     loads["scalar"].wait()
     for z in range(8):
@@ -420,11 +420,11 @@
         back_in_x(0, c)
         for i in (c, c + 3):
             sent_a(0, i)
-        x_forward(1, c)
+        x_forward(1, c, 0)
         sent(0, c)
 
     each(3, middle)
-    each(3, lambda c: send_a(1, c + 3))
+    each(3, lambda c: x_forward(1, c, 1))
     spectral(1, second)
 
     def coefficients(z, c):
@@ -482,11 +482,8 @@
                 zsend[s + 1, 1, cells] = top.astype(BF)
                 send_z(s + 1, q)
 
-            def inner(z, _):
+            for z in range(2, 8):
                 block(z, q, state[now, z - 1, rows], state[now, z + 1, rows])
-                return _
-
-            lax.fori_loop(2, 8, inner, 0)
             if q in (0, 3):
                 side = q // 3
 
@@ -510,6 +507,19 @@
     for c in range(3):
         pltpu.make_async_copy(field.at[c], velocity_h.at[c], out_sem.at[c]).wait()
     out.wait()
+
+
+def place_kernel(velocity_in, conc_in, velocity, conc, held, in_sem, out_sem):
+    pairs = [(velocity_in.at[c], held.at[c], velocity.at[c]) for c in range(3)] + [(conc_in, held.at[3], conc)]
+    loads = [pltpu.make_async_copy(a, b, in_sem.at[i]) for i, (a, b, _) in enumerate(pairs)]
+    stores = [pltpu.make_async_copy(b, c, out_sem.at[i]) for i, (_, b, c) in enumerate(pairs)]
+    for copy in loads:
+        copy.start()
+    for load, store in zip(loads, stores):
+        load.wait()
+        store.start()
+    for copy in stores:
+        copy.wait()
 
 
 def local(force, mask, scalar):
@@ -557,7 +567,17 @@
         scalar,
         *[jnp.asarray(tables[name]) for name in TABLES],
     )
-    return velocity, conc
+    return pl.pallas_call(
+        place_kernel,
+        out_shape=(
+            jax.ShapeDtypeStruct((3, 8, 64, 512), BF),
+            jax.ShapeDtypeStruct((8, 64, 512), BF),
+        ),
+        in_specs=[any_spec] * 2,
+        out_specs=(any_spec, any_spec),
+        scratch_shapes=[vm((4, 8, 64, 512), BF), dma((4,)), dma((4,))],
+        name="place",
+    )(velocity, conc)
 
 
 def solution(mesh):

time: 146 us -> 145 us (level)
  local copies, waits for them, and re-layouts: 3.56 us -> 0 us
  Pallas kernels: 142 us -> 144 us
    unnamed x4 -> x0, local copies, waits for them, and re-layouts: 3.56 us -> none
    pallas_call x0 -> x1, Pallas kernels: none -> 2.42 us  [local(): pl.pallas_call(place_kernel, out_shape=(jax.ShapeDtypeStruct((3, 8, 64, 5...]
where the time goes in v2:
time: 145 us; the launch traced here: 144 us
  Pallas kernels  144 us (99%)
    pallas_call x1, Pallas kernels, local(): pl.pallas_call(mixer_kernel, out_shape=(jax.ShapeDtypeStruct((3, 8, 64, 5...  141 us

profile of v2, /device:TPU:0, one launch (start us, length us, event | category | flops | bytes accessed | tf_op | source)
XLA Modules:
  0.0 144.5 jit_solution(1027309980910094186)
XLA Ops:
  0.6 141.4 %mixer.1 = (bf16[3,8,64,512]{3,2,1,0:T(8,128)(2,1)}, bf16[8,64,512]{2,1,0:T(8,128)(2,1)}) custom-call(bf16[3,8,64,512]{3,2,1,0:T(8,128)(2,1)} %refs_0_.1, s32[8,64,512]{2,1,0:T(8,128)} %refs_1_.1, bf16[8,64,512]{2,1,0:T(8,128)(2,1)} %refs_2_.1, bf16[512,512]{1,0:T(8,128)(2,1)} %constant.14.clone.refs_3_, bf16[512,512]{1,0:T(8,128)(2,1)} %constant.15.clone.refs_4_, ...), custom_call_target="tpu_custom_call" | custom-call | tf_op jit(solution)/shard_map/mixer/pallas_call | solution.py:551
  142.1 2.4 %place.1 = (bf16[3,8,64,512]{3,2,1,0:T(8,128)(2,1)}, bf16[8,64,512]{2,1,0:T(8,128)(2,1)}) custom-call(bf16[3,8,64,512]{3,2,1,0:T(8,128)(2,1)} %get-tuple-element.4.velocity_in, bf16[8,64,512]{2,1,0:T(8,128)(2,1)} %get-tuple-element.5.conc_in), custom_call_target="tpu_custom_call" | custom-call | tf_op jit(solution)/shard_map/place/pallas_call | solution.py:570

commit v3 on v2

--- a/solution.py
+++ b/solution.py
@@ -23,9 +23,10 @@
         return values.astype(np.float32).astype(ml_dtypes.bfloat16)
 
     x = np.arange(512)
-    h, ri, d, k = np.meshgrid(np.arange(2), np.arange(2), np.arange(8), np.arange(16), indexing="ij")
-    m = (d * 32 + h * 16 + k).reshape(-1)
-    ri = ri.reshape(-1)
+    ri, d, k = (v.reshape(-1) for v in np.meshgrid(np.arange(2), np.arange(8), np.arange(16), indexing="ij"))
+    e1, ri1, k1 = (v.reshape(-1) for v in np.meshgrid(np.arange(16), np.arange(2), np.arange(8), indexing="ij"))
+    m = np.concatenate([d * 32 + k, (e1 // 2) * 32 + 16 + (e1 % 2) * 8 + k1])
+    ri = np.concatenate([ri, ri1])
     angle = (np.outer(x, m) % 512) * (TWO_PI / 512)
     fx = np.where(ri == 0, np.cos(angle), -np.sin(angle)) / np.sqrt(512.0)
     bx = (fx * np.where(m == 0, 1.0, 2.0)).T
@@ -35,6 +36,8 @@
     real = np.concatenate([c, s], 1).reshape(16, 1, 16, 512)
     imag = np.concatenate([-s, c], 1).reshape(16, 1, 16, 512)
     ty = np.concatenate([real, imag], 1).reshape(512, 512)
+    uy = np.concatenate([c, s], 1)
+    uyi = np.concatenate([c, -s], 1)
     n = np.arange(16)
     angle = (np.outer(n, n) % 16) * (TWO_PI / 16)
     c, s = np.cos(angle) / 4.0, np.sin(angle) / 4.0
@@ -54,14 +57,33 @@
                     csi[d, k2 * 16 + k, 256 + at + k] = s[zp, k2]
                 tw[d, 0, :, at : at + 16] = np.cos(TWO_PI * zp * n / 256)[:, None] / 4.0
                 tw[d, 1, :, at : at + 16] = np.sin(TWO_PI * zp * n / 256)[:, None] / 4.0
+    utw = np.zeros((16, 2, 16, 128))
+    uz = np.zeros((8, 256, 256))
+    k = np.arange(8)
+    for turn in range(8):
+        for low in range(2):
+            for p in range(8):
+                zp = low * 8 + (p - turn) % 8
+                utw[low * 8 + turn, 0, :, p * 16 : p * 16 + 16] = np.cos(TWO_PI * zp * n / 256)[:, None] / 4.0
+                utw[low * 8 + turn, 1, :, p * 16 : p * 16 + 16] = np.sin(TWO_PI * zp * n / 256)[:, None] / 4.0
+                at = low * 128 + p * 16
+                for k2 in range(16):
+                    to = k2 * 16
+                    uz[turn, at + k, to + k] = c[zp, k2]
+                    uz[turn, at + 8 + k, to + k] = s[zp, k2]
+                    uz[turn, at + k, to + 8 + k] = -s[zp, k2]
+                    uz[turn, at + 8 + k, to + 8 + k] = c[zp, k2]
     return dict(
+        uy=half(uy), uyi=half(uyi), uz=half(uz), uzi=half(uz.transpose(0, 2, 1)), utw=utw.astype(np.float32),
         fx=half(fx), bx=half(bx), ty=half(ty), tyi=half(ty.T), cs=half(cs), csi=half(csi),
         tw=tw.astype(np.float32),
     )
 
 
-TABLES = ("fx", "ty", "tw", "cs", "csi", "tyi", "bx")
-ROTATED = ("cs", "tw", "csi")
+TABLES = ("fx", "ty", "utw", "tw", "cs", "uy", "uz", "csi", "uzi", "tyi", "uyi", "bx")
+BY_D = ("cs", "tw", "csi")
+BY_E = ("uz", "uzi")
+VARIED = BY_D + BY_E + ("utw",)
 
 
 def radix4(a, sign):
@@ -83,6 +105,35 @@
     c, s = float(np.cos(TWO_PI * j / 16)), float(np.sin(TWO_PI * j / 16)) * sign
     re, im = value
     return re * c + im * s, im * c - re * s
+
+
+def times_minus_i(value):
+    imag = (lax.broadcasted_iota(jnp.int32, value.shape, 1) & 8) != 0
+    return jnp.where(imag, -pltpu.roll(value, 8, 1), pltpu.roll(value, 120, 1))
+
+
+def packed_radix4(a, sign):
+    t0, t1, t2 = a[0] + a[2], a[0] - a[2], a[1] + a[3]
+    t3 = times_minus_i(a[1] - a[3])
+    if sign < 0:
+        t3 = -t3
+    return t0 + t2, t1 + t3, t0 - t2, t1 - t3
+
+
+def packed_turned(value, j, sign):
+    if j == 0:
+        return value
+    c, s = float(np.cos(TWO_PI * j / 16)), float(np.sin(TWO_PI * j / 16)) * sign
+    return value * c + times_minus_i(value) * s
+
+
+def packed_dft16(values, sign):
+    parts = [packed_radix4(values[low::4], sign) for low in range(4)]
+    parts = [[packed_turned(v, low * k, sign) for k, v in enumerate(parts[low])] for low in range(4)]
+    out = [None] * 16
+    for k in range(4):
+        out[k::4] = packed_radix4([parts[low][k] for low in range(4)], sign)
+    return out
 
 
 def merge(tiles, place):
@@ -104,6 +155,8 @@
     (field, mask, scalar, *rest) = refs[5 + count :]
     tab = dict(zip(TABLES, rest[:count]))
     (gain, inv, sa, ra, sb, rb, sbi, rbi, sai, rai, spec, first, second, lines, big, mid,
+     gain1, inv1, su, ru, sv, rv, svi, rvi, sui, rui, spec1, first1, second1, stacked,
+     u_send, u_recv, v_send, v_recv,
      zsend, zrecv, ysend, yrecv, coef, state, conc,
      in_sem, tab_sem, a_send, a_recv, b_send, b_recv, z_ssem, z_rsem, y_ssem, y_rsem, out_sem) = rest[count:]
 
@@ -121,7 +174,9 @@
     def load_table(name):
         source = tables_h[name]
         sem = tab_sem.at[TABLES.index(name)]
-        return load(source.at[d] if name in ROTATED else source, tab[name], sem)
+        if name in VARIED:
+            source = source.at[d if name in BY_D else (e & 7) + (8 * xl if name == "utw" else 0)]
+        return load(source, tab[name], sem)
 
     loads = {0: load(force_h.at[0], field.at[0], in_sem.at[0]), "fx": load_table("fx")}
     for i in (1, 2):
@@ -203,16 +258,47 @@
             remote(slab, target, b_send.at[k, i], recv, device).start()
         pltpu.make_async_copy(source.at[i, my_slab], target, recv).start()
 
+    def send_u(source, into, k, t, c):
+        target = into.at[t, c, e]
+        recv = u_recv.at[k, c]
+        for to, device in plane_peers:
+            remote(source.at[c, to], target, u_send.at[k, c], recv, device).start()
+        pltpu.make_async_copy(source.at[c, e], target, recv).start()
+
+    def send_v(t, c):
+        target = rv.at[t, c, :, my_rows, my_lanes]
+        recv = v_recv.at[2 * t, c]
+        for to, device in x_peers:
+            remote(sv.at[c, pl.ds(2 * to, 2)], target, v_send.at[2 * t, c], recv, device).start()
+        pltpu.make_async_copy(sv.at[c, pl.ds(2 * d, 2)], target, recv).start()
+
+    def send_vi(t, c):
+        target = rvi.at[t, c, pl.ds(2 * d, 2)]
+        recv = v_recv.at[2 * t + 1, c]
+
+        def piece(to):
+            rows = pl.ds(pl.multiple_of((to & 3) * 64, 64), 64)
+            lanes = pl.ds(pl.multiple_of((to // 4) * 128, 128), 128)
+            return svi.at[c, :, rows, lanes]
+
+        for to, device in x_peers:
+            remote(piece(to), target, v_send.at[2 * t + 1, c], recv, device).start()
+        pltpu.make_async_copy(piece(d), target, recv).start()
+
     def arrived(buffer, sem):
         pltpu.make_async_copy(buffer, buffer, sem).wait()
 
     def sent_a(k, i):
-        part = sa.at[i, pl.ds(0, 7)]
-        pltpu.make_async_copy(part, part, a_send.at[k, i]).wait()
+        arrived(sa.at[i, pl.ds(0, 7)], a_send.at[k, i])
 
     def sent_b(k, i):
-        part = sb.at[i, pl.ds(0, 480)]
-        pltpu.make_async_copy(part, part, b_send.at[k, i]).wait()
+        arrived(sb.at[i, pl.ds(0, 480)], b_send.at[k, i])
+
+    def sent_u(k, i):
+        arrived(su.at[i, pl.ds(0, 15)], u_send.at[k, i])
+
+    def sent_v(k, i):
+        arrived(sv.at[i, pl.ds(0, 14)], v_send.at[k, i])
 
     def send_z(s, q):
         rows = pl.ds(16 * q, 16)
@@ -226,8 +312,8 @@
 
     place = lax.broadcasted_iota(jnp.int32, (64, 128), 1) // 16
 
-    def x_forward(t, c, h):
-        spread = dot(field[c].reshape(512, 512), tab["fx"][:, h * 256 : h * 256 + 256])
+    def x_forward(t, c):
+        spread = dot(field[c].reshape(512, 512), tab["fx"][:, 0:256])
         for ri in range(2):
             tiles = []
             for z in range(8):
@@ -235,12 +321,27 @@
                 tiles.append(pltpu.roll(tile, 16 * z, 1) if z else tile)
             tiles = merge(tiles, place)
             for to in range(8):
-                sa[3 * h + c, to, ri] = tiles[-to % 8].astype(BF)
-        send_a(t, 3 * h + c)
+                sa[c, to, ri] = tiles[-to % 8].astype(BF)
+        send_a(t, c)
+
+    def x_forward1(t, c):
+        spread = dot(field[c].reshape(512, 512), tab["fx"][:, 256:512])
+        for j in range(2):
+            tiles = []
+            for z in range(8):
+                tile = spread[z * 64 : z * 64 + 64, j * 128 : j * 128 + 128]
+                tiles.append(pltpu.roll(tile, 16 * z, 1) if z else tile)
+            tiles = merge(tiles, place)
+            for to in range(8):
+                su[c, 8 * j + to] = tiles[-to % 8].astype(BF)
+        send_u(su, ru, 2 * t, t, c)
 
     def x_inverse(t, c):
         for j in range(4):
-            tiles = [rai[t, 3 * (j // 2) + c, source, j % 2].astype(F32) for source in range(8)]
+            if j < 2:
+                tiles = [rai[t, c, source, j].astype(F32) for source in range(8)]
+            else:
+                tiles = [rui[t, c, 8 * (j - 2) + source].astype(F32) for source in range(8)]
             tiles = merge(tiles, place)
             for z in range(8):
                 tile = tiles[-z % 8]
@@ -309,48 +410,127 @@
                     sbi[i, to + 16 : to + 32, lanes] = im.astype(BF)
         send_b(sbi, rbi, 2 * t + 1, t, i)
 
+    def v_forward(t, c):
+        arrived(ru.at[t, c], u_recv.at[2 * t, c])
+
+        def some(n, carry):
+            rows = pl.ds(pl.multiple_of(n * 16, 16), 16)
+            out = packed_dft16([ru[t, c, j, rows].astype(F32) for j in range(16)], 1)
+            for k1, value in enumerate(out):
+                wc, ws = tab["utw"][0, k1 : k1 + 1], tab["utw"][1, k1 : k1 + 1]
+                sv[c, k1, rows] = (value * wc + times_minus_i(value) * ws).astype(BF)
+            return carry
+
+        lax.fori_loop(0, 4, some, 0)
+        send_v(t, c)
+
+    def v_inverse(t, c):
+        arrived(rvi.at[t, c], v_recv.at[2 * t + 1, c])
+
+        def some(n, carry):
+            rows = pl.ds(pl.multiple_of(n * 16, 16), 16)
+            values = []
+            for k1 in range(16):
+                value = rvi[t, c, k1, rows].astype(F32)
+                wc, ws = tab["utw"][0, k1 : k1 + 1], tab["utw"][1, k1 : k1 + 1]
+                values.append(value * wc - times_minus_i(value) * ws)
+            for j, value in enumerate(packed_dft16(values, -1)):
+                sui[c, j, rows] = value.astype(BF)
+            return carry
+
+        lax.fori_loop(0, 4, some, 0)
+        send_u(sui, rui, 2 * t + 1, t, c)
+
+    def y_product(table, values, wide):
+        for half in range(2):
+            lanes = slice(half * 128, half * 128 + 128)
+            stacked[256:512, lanes] = times_minus_i(wide[:, lanes]).astype(BF)
+        stacked[0:256, :] = values
+        return dot(table, stacked[...]).astype(BF)
+
+    def w_forward(t, c):
+        arrived(rv.at[t, c], v_recv.at[2 * t, c])
+        for k1 in range(2):
+            values = rv[t, c, k1]
+            big[k1 * 256 : k1 * 256 + 256, :] = y_product(tab["uy"][...], values, values.astype(F32))
+        spec1[c] = dot(big[...], tab["uz"][...])
+
+    def w_inverse(source, t, c):
+        wide = dot(source[c], tab["uzi"][...])
+        for k1 in range(2):
+            part = wide[k1 * 256 : k1 * 256 + 256]
+            svi[c, k1] = y_product(tab["uyi"][...], part.astype(BF), part)
+        send_vi(t, c)
+
     lane = lax.broadcasted_iota(jnp.int32, (16, 256), 1)
     unit_long, unit = np.float32(TWO_PI / 512), np.float32(TWO_PI / 256)
     index_y = e * 16 + lax.broadcasted_iota(jnp.int32, (16, 256), 0)
     wave_y = jnp.where(index_y < 128, index_y, index_y - 256).astype(F32) * unit
 
-    def along_x(h):
-        return (d * 32 + h * 16 + (lane & 15)).astype(F32) * unit_long
+    wave_x = (d * 32 + (lane & 15)).astype(F32) * unit_long
+    wave_x1 = ((e // 2) * 32 + 16 + (e & 1) * 8 + (lane & 7)).astype(F32) * unit_long
 
     def along_z(k1):
         index_z = k1 + 16 * (lane // 16)
         return index_z, jnp.where(index_z < 128, index_z, index_z - 256).astype(F32) * unit
 
-    def factors(step, _):
-        h, k1 = step // 16, step & 15
-        wave_x = along_x(h)
-        index_z, wave_z = along_z(k1)
-        ksq = wave_x * wave_x + wave_y * wave_y + wave_z * wave_z
-        edge = (index_y == 128) | (index_z == 128)
-        rows = pl.ds(pl.multiple_of(k1 * 16, 16), 16)
-        gain[h, rows] = jnp.where(edge, 0.0, 1.0 / (0.05 * ksq + 0.5))
-        inv[h, rows] = jnp.where(ksq > 0.0, 1.0 / jnp.where(ksq > 0.0, ksq, 1.0), 0.0)
-        return _
-
-    def project(t, h):
-        wave_x = along_x(h)
-
-        def one(k1, _):
-            wave_z = along_z(k1)[1]
-            rows = pl.ds(pl.multiple_of(k1 * 16, 16), 16)
-            g, n = gain[h, rows], inv[h, rows]
+    def at_rows(n):
+        return pl.ds(pl.multiple_of(n * 16, 16), 16)
+
+    def along_y1(n):
+        index = (n & 15) * 16 + lax.broadcasted_iota(jnp.int32, (16, 256), 0)
+        return index, jnp.where(index < 128, index, index - 256).astype(F32) * unit
+
+    def scales(kx, ky, kz, edge):
+        ksq = kx * kx + ky * ky + kz * kz
+        return (
+            jnp.where(edge, 0.0, 1.0 / (0.05 * ksq + 0.5)),
+            jnp.where(ksq > 0.0, 1.0 / jnp.where(ksq > 0.0, ksq, 1.0), 0.0),
+        )
+
+    def factors(n, carry):
+        index_z, wave_z = along_z(n)
+        gain[at_rows(n)], inv[at_rows(n)] = scales(wave_x, wave_y, wave_z, (index_y == 128) | (index_z == 128))
+        return carry
+
+    def factors1(n, carry):
+        index_z, wave_z = along_z(2 * d + n // 16)
+        index, wave = along_y1(n)
+        gain1[at_rows(n)], inv1[at_rows(n)] = scales(wave_x1, wave, wave_z, (index == 128) | (index_z == 128))
+        return carry
+
+    def projected(w, waves, g, n):
+        along = (waves[0] * w[0] + waves[1] * w[1] + waves[2] * w[2]) * n
+        return [g * (w[c] - waves[c] * along) for c in range(3)]
+
+    def project(t):
+        def one(n, carry):
+            rows = at_rows(n)
+            waves = (wave_x, wave_y, along_z(n)[1])
             for ri in range(2):
-                w = [spec[3 * h + c, ri, rows] for c in range(3)]
-                along = (wave_x * w[0] + wave_y * w[1] + wave_z * w[2]) * n
-                for c, wave in enumerate((wave_x, wave_y, wave_z)):
-                    value = g * (w[c] - wave * along)
+                out = projected([spec[c, ri, rows] for c in range(3)], waves, gain[rows], inv[rows])
+                for c in range(3):
                     if t == 0:
-                        first[3 * h + c, ri, rows] = value.astype(BF)
+                        first[c, ri, rows] = out[c].astype(BF)
                     else:
-                        second[3 * h + c, ri, rows] = (first[3 * h + c, ri, rows].astype(F32) - value).astype(BF)
-            return _
+                        second[c, ri, rows] = (first[c, ri, rows].astype(F32) - out[c]).astype(BF)
+            return carry
 
         lax.fori_loop(0, 16, one, 0)
+
+    def project1(t):
+        def one(n, carry):
+            rows = at_rows(n)
+            waves = (wave_x1, along_y1(n)[1], along_z(2 * d + n // 16)[1])
+            out = projected([spec1[c, rows] for c in range(3)], waves, gain1[rows], inv1[rows])
+            for c in range(3):
+                if t == 0:
+                    first1[c, rows] = out[c].astype(BF)
+                else:
+                    second1[c, rows] = (first1[c, rows].astype(F32) - out[c]).astype(BF)
+            return carry
+
+        lax.fori_loop(0, 32, one, 0)
 
     def each(count, step):
         def body(i, _):
@@ -359,36 +539,40 @@
 
         lax.fori_loop(0, count, body, 0)
 
-    def spectral(t, source):
-        def step(n):
-            @pl.when(n < 6)
-            def _():
-                y_forward(t, n)
-
-            @pl.when(((n >= 1) & (n <= 3)) | ((n >= 6) & (n <= 8)))
-            def _():
-                z_forward(t, jnp.where(n <= 3, n - 1, n - 3))
-
-            @pl.when((n == 3) | (n == 8))
-            def _():
-                project(t, jnp.where(n == 3, 0, 1))
-
-            @pl.when((n == 3) | (n == 5) | (n == 6) | ((n >= 8) & (n <= 10)))
-            def _():
-                z_inverse(source, t, jnp.where(n == 3, 0, jnp.where(n <= 6, n - 4, n - 5)))
-
-            @pl.when((n == 5) | (n >= 8))
-            def _():
-                y_inverse(t, jnp.where(n == 5, 0, n - 7))
-
-        each(13, step)
+    def spectral(t, source, source1):
+        def out(c):
+            y_forward(t, c)
+            v_forward(t, c)
+
+        def inner(c):
+            w_forward(t, c)
+            z_forward(t, c)
+
+        def outer(c):
+            w_inverse(source1, t, c)
+            z_inverse(source, t, c)
+
+        def back(c):
+            v_inverse(t, c)
+            y_inverse(t, c)
+
+        each(3, out)
+        each(3, inner)
+        project1(t)
+        project(t)
+        each(3, outer)
+        each(3, back)
 
     loads["fx"].wait()
     for i in range(3):
         loads[i].wait()
-    each(3, lambda c: x_forward(0, c, 0))
-    each(3, lambda c: x_forward(0, c, 1))
-    lax.fori_loop(0, 32, factors, 0)
+    def start(c):
+        x_forward(0, c)
+        x_forward1(0, c)
+
+    each(3, start)
+    lax.fori_loop(0, 16, factors, 0)
+    lax.fori_loop(0, 32, factors1, 0)
     loads["scalar"].wait()
     for z in range(8):
         state[0, z + 1, pl.ds(8, 64), :] = scalar[z].astype(F32)
@@ -403,29 +587,28 @@
     for name in TABLES[1:]:
         loads[name].wait()
     loads["mask"].wait()
-    spectral(0, first)
+    spectral(0, first, first1)
 
     def back_in_x(t, c):
-        for i in (c, c + 3):
-            arrived(rai.at[t, i], a_recv.at[2 * t + 1, i])
+        arrived(rai.at[t, c], a_recv.at[2 * t + 1, c])
+        arrived(rui.at[t, c], u_recv.at[2 * t + 1, c])
         x_inverse(t, c)
 
     def sent(t, c):
-        for i in (c, c + 3):
-            sent_b(2 * t, i)
-            sent_b(2 * t + 1, i)
-            sent_a(2 * t + 1, i)
+        for k in (2 * t, 2 * t + 1):
+            sent_a(k, c)
+            sent_b(k, c)
+            sent_u(k, c)
+            sent_v(k, c)
 
     def middle(c):
         back_in_x(0, c)
-        for i in (c, c + 3):
-            sent_a(0, i)
-        x_forward(1, c, 0)
         sent(0, c)
+        x_forward(1, c)
+        x_forward1(1, c)
 
     each(3, middle)
-    each(3, lambda c: x_forward(1, c, 1))
-    spectral(1, second)
+    spectral(1, second, second1)
 
     def coefficients(z, c):
         fluid = 0.25 * (1.0 - mask[z].astype(F32))
@@ -442,8 +625,6 @@
         back_in_x(1, c)
         pltpu.make_async_copy(field.at[c], velocity_h.at[c], out_sem.at[c]).start()
         lax.fori_loop(0, 8, coefficients, c)
-        for i in (c, c + 3):
-            sent_a(2, i)
         sent(1, c)
 
     each(3, last)
@@ -529,21 +710,29 @@
     scratch = [vm((3, 8, 64, 512), BF), vm((8, 64, 512), jnp.int32), vm((8, 64, 512), BF)]
     for name in TABLES:
         value = tables[name]
-        shape = value.shape[1:] if name in ROTATED else value.shape
+        shape = value.shape[1:] if name in VARIED else value.shape
         scratch.append(vm(shape, value.dtype))
     scratch += [
-        vm((2, 256, 256), F32), vm((2, 256, 256), F32),
-        vm((6, 8, 2, 64, 128), BF), vm((2, 6, 2, 256, 256), BF),
-        vm((6, 512, 256), BF), vm((2, 6, 512, 256), BF),
-        vm((6, 512, 256), BF), vm((2, 6, 512, 256), BF),
-        vm((6, 2, 256, 256), BF), vm((2, 6, 8, 2, 64, 128), BF),
-        vm((6, 2, 256, 256), F32), vm((6, 2, 256, 256), BF), vm((6, 2, 256, 256), BF),
+        vm((256, 256), F32), vm((256, 256), F32),
+        vm((3, 8, 2, 64, 128), BF), vm((2, 3, 2, 256, 256), BF),
+        vm((3, 512, 256), BF), vm((2, 3, 512, 256), BF),
+        vm((3, 512, 256), BF), vm((2, 3, 512, 256), BF),
+        vm((3, 2, 256, 256), BF), vm((2, 3, 8, 2, 64, 128), BF),
+        vm((3, 2, 256, 256), F32), vm((3, 2, 256, 256), BF), vm((3, 2, 256, 256), BF),
         vm((512, 512), BF), vm((512, 256), BF), vm((4, 4, 2, 16, 256), F32),
+        vm((512, 256), F32), vm((512, 256), F32),
+        vm((3, 16, 64, 128), BF), vm((2, 3, 16, 64, 128), BF),
+        vm((3, 16, 64, 128), BF), vm((2, 3, 2, 256, 256), BF),
+        vm((3, 2, 256, 256), BF), vm((2, 3, 16, 64, 128), BF),
+        vm((3, 16, 64, 128), BF), vm((2, 3, 16, 64, 128), BF),
+        vm((3, 512, 256), F32), vm((3, 512, 256), BF), vm((3, 512, 256), BF),
+        vm((512, 256), BF),
+        dma((4, 3)), dma((4, 3)), dma((4, 3)), dma((4, 3)),
         vm((SECTIONS, 2, 64, 512), BF), vm((SECTIONS, 2, 64, 512), BF),
         vm((SECTIONS, 2, 8, 512), F32), vm((SECTIONS, 2, 8, 512), F32),
         vm((7, 8, 64, 512), F32), vm((2, 10, 80, 512), F32), vm((8, 64, 512), BF),
         dma((5,)), dma((len(TABLES),)),
-        dma((4, 6)), dma((4, 6)), dma((4, 6)), dma((4, 6)),
+        dma((4, 3)), dma((4, 3)), dma((4, 3)), dma((4, 3)),
         dma((SECTIONS, 2)), dma((SECTIONS, 2, 4)), dma((SECTIONS, 2)), dma((SECTIONS, 2)),
         dma((4,)),
     ]

time: 145 us -> 127 us (0.88)
  Pallas kernels: 144 us -> 126 us
    pallas_call x1, Pallas kernels: 141 us -> 123 us  [local(): pl.pallas_call(mixer_kernel, out_shape=(jax.ShapeDtypeStruct((3, 8, 64, 5...]
where the time goes in v3:
time: 127 us; the launch traced here: 126 us
  Pallas kernels  126 us (99%)
    pallas_call x1, Pallas kernels, local(): pl.pallas_call(mixer_kernel, out_shape=(jax.ShapeDtypeStruct((3, 8, 64, 5...  123 us

profile of v3, /device:TPU:0, one launch (start us, length us, event | category | flops | bytes accessed | tf_op | source)
XLA Modules:
  0.0 126.4 jit_solution(11781384176012594776)
XLA Ops:
  0.6 123.4 %mixer.1 = (bf16[3,8,64,512]{3,2,1,0:T(8,128)(2,1)}, bf16[8,64,512]{2,1,0:T(8,128)(2,1)}) custom-call(bf16[3,8,64,512]{3,2,1,0:T(8,128)(2,1)} %refs_0_.1, s32[8,64,512]{2,1,0:T(8,128)} %refs_1_.1, bf16[8,64,512]{2,1,0:T(8,128)(2,1)} %refs_2_.1, bf16[512,512]{1,0:T(8,128)(2,1)} %constant.24.clone.refs_3_, bf16[512,512]{1,0:T(8,128)(2,1)} %constant.25.clone.refs_4_, ...), custom_call_target="tpu_custom_call" | custom-call | tf_op jit(solution)/shard_map/mixer/pallas_call | solution.py:740
  124.0 2.4 %place.1 = (bf16[3,8,64,512]{3,2,1,0:T(8,128)(2,1)}, bf16[8,64,512]{2,1,0:T(8,128)(2,1)}) custom-call(bf16[3,8,64,512]{3,2,1,0:T(8,128)(2,1)} %get-tuple-element.4.velocity_in, bf16[8,64,512]{2,1,0:T(8,128)(2,1)} %get-tuple-element.5.conc_in), custom_call_target="tpu_custom_call" | custom-call | tf_op jit(solution)/shard_map/place/pallas_call | solution.py:759

commit v4 on v3

--- a/solution.py
+++ b/solution.py
@@ -155,9 +155,9 @@
     (field, mask, scalar, *rest) = refs[5 + count :]
     tab = dict(zip(TABLES, rest[:count]))
     (gain, inv, sa, ra, sb, rb, sbi, rbi, sai, rai, spec, first, second, lines, big, mid,
-     gain1, inv1, su, ru, sv, rv, svi, rvi, sui, rui, spec1, first1, second1, stacked,
+     gain1, inv1, su, ru, sv, rv, svi, rvi, sui, rui, spec1, first1, second1, stacked, dots, dots1, summed,
      u_send, u_recv, v_send, v_recv,
-     zsend, zrecv, ysend, yrecv, coef, state, conc,
+     zsend, zrecv, ysend, yrecv, edge, coef, state, conc,
      in_sem, tab_sem, a_send, a_recv, b_send, b_recv, z_ssem, z_rsem, y_ssem, y_rsem, out_sem) = rest[count:]
 
     r = lax.axis_index("row")
@@ -305,6 +305,10 @@
         for side, device in ((0, z_down), (1, z_up)):
             remote(zsend.at[s, side, rows], zrecv.at[s, 1 - side, rows],
                    z_ssem.at[s, side], z_rsem.at[s, 1 - side, q], device).start()
+
+    def pack_edge(s, side):
+        value = edge[...]
+        ysend[s, side] = jnp.concatenate([value[:, 0:256], value[:, 256:512]], axis=0).astype(BF)
 
     def send_y(s, side):
         remote(ysend.at[s, side], yrecv.at[s, 1 - side], y_ssem.at[s, side], y_rsem.at[s, 1 - side],
@@ -337,7 +341,7 @@
         send_u(su, ru, 2 * t, t, c)
 
     def x_inverse(t, c):
-        for j in range(4):
+        def gather(j):
             if j < 2:
                 tiles = [rai[t, c, source, j].astype(F32) for source in range(8)]
             else:
@@ -347,7 +351,15 @@
                 tile = tiles[-z % 8]
                 tile = pltpu.roll(tile, 128 - 16 * z, 1) if z else tile
                 lines[z * 64 : z * 64 + 64, j * 128 : j * 128 + 128] = tile.astype(BF)
-        values = dot(lines[...], tab["bx"][...]).astype(BF).reshape(8, 64, 512)
+
+        arrived(rai.at[t, c], a_recv.at[2 * t + 1, c])
+        gather(0)
+        gather(1)
+        summed[...] = dot(lines[:, 0:256], tab["bx"][0:256, :])
+        arrived(rui.at[t, c], u_recv.at[2 * t + 1, c])
+        gather(2)
+        gather(3)
+        values = (summed[...] + dot(lines[:, 256:512], tab["bx"][256:512, :])).astype(BF).reshape(8, 64, 512)
         if t == 0:
             values = (values.astype(F32) * mask[...].astype(F32)).astype(BF)
         field[c] = values
@@ -499,35 +511,70 @@
         gain1[at_rows(n)], inv1[at_rows(n)] = scales(wave_x1, wave, wave_z, (index == 128) | (index_z == 128))
         return carry
 
-    def projected(w, waves, g, n):
-        along = (waves[0] * w[0] + waves[1] * w[1] + waves[2] * w[2]) * n
-        return [g * (w[c] - waves[c] * along) for c in range(3)]
-
-    def project(t):
+    def parts():
+        def one(n, carry):
+            rows = at_rows(n)
+            for ri in range(2):
+                dots[ri, rows] = wave_x * spec[0, ri, rows] + wave_y * spec[1, ri, rows]
+            return carry
+
+        lax.fori_loop(0, 16, one, 0)
+
+    def keep(t, kept, result, at, value):
+        if t == 0:
+            kept[at] = value.astype(BF)
+        else:
+            result[at] = (kept[at].astype(F32) - value).astype(BF)
+
+    def project_x(t):
+        def one(n, carry):
+            rows = at_rows(n)
+            wave_z = along_z(n)[1]
+            for ri in range(2):
+                along = (dots[ri, rows] + wave_z * spec[2, ri, rows]) * inv[rows]
+                dots[ri, rows] = along
+                keep(t, first, second, (0, ri, rows), gain[rows] * (spec[0, ri, rows] - wave_x * along))
+            return carry
+
+        lax.fori_loop(0, 16, one, 0)
+
+    def project_yz(t):
         def one(n, carry):
             rows = at_rows(n)
             waves = (wave_x, wave_y, along_z(n)[1])
             for ri in range(2):
-                out = projected([spec[c, ri, rows] for c in range(3)], waves, gain[rows], inv[rows])
-                for c in range(3):
-                    if t == 0:
-                        first[c, ri, rows] = out[c].astype(BF)
-                    else:
-                        second[c, ri, rows] = (first[c, ri, rows].astype(F32) - out[c]).astype(BF)
+                along = dots[ri, rows]
+                for c in (1, 2):
+                    keep(t, first, second, (c, ri, rows), gain[rows] * (spec[c, ri, rows] - waves[c] * along))
             return carry
 
         lax.fori_loop(0, 16, one, 0)
 
-    def project1(t):
+    def parts1():
+        def one(n, carry):
+            rows = at_rows(n)
+            dots1[rows] = wave_x1 * spec1[0, rows] + along_y1(n)[1] * spec1[1, rows]
+            return carry
+
+        lax.fori_loop(0, 32, one, 0)
+
+    def project1_x(t):
+        def one(n, carry):
+            rows = at_rows(n)
+            along = (dots1[rows] + along_z(2 * d + n // 16)[1] * spec1[2, rows]) * inv1[rows]
+            dots1[rows] = along
+            keep(t, first1, second1, (0, rows), gain1[rows] * (spec1[0, rows] - wave_x1 * along))
+            return carry
+
+        lax.fori_loop(0, 32, one, 0)
+
+    def project1_yz(t):
         def one(n, carry):
             rows = at_rows(n)
             waves = (wave_x1, along_y1(n)[1], along_z(2 * d + n // 16)[1])
-            out = projected([spec1[c, rows] for c in range(3)], waves, gain1[rows], inv1[rows])
-            for c in range(3):
-                if t == 0:
-                    first1[c, rows] = out[c].astype(BF)
-                else:
-                    second1[c, rows] = (first1[c, rows].astype(F32) - out[c]).astype(BF)
+            along = dots1[rows]
+            for c in (1, 2):
+                keep(t, first1, second1, (c, rows), gain1[rows] * (spec1[c, rows] - waves[c] * along))
             return carry
 
         lax.fori_loop(0, 32, one, 0)
@@ -549,18 +596,26 @@
             z_forward(t, c)
 
         def outer(c):
-            w_inverse(source1, t, c)
-            z_inverse(source, t, c)
+            w_inverse(source1, t, c + 1)
+            z_inverse(source, t, c + 1)
 
         def back(c):
             v_inverse(t, c)
             y_inverse(t, c)
 
         each(3, out)
-        each(3, inner)
-        project1(t)
-        project(t)
-        each(3, outer)
+        each(2, inner)
+        parts1()
+        parts()
+        w_forward(t, 2)
+        project1_x(t)
+        w_inverse(source1, t, 0)
+        z_forward(t, 2)
+        project_x(t)
+        z_inverse(source, t, 0)
+        project1_yz(t)
+        project_yz(t)
+        each(2, outer)
         each(3, back)
 
     loads["fx"].wait()
@@ -576,23 +631,19 @@
     loads["scalar"].wait()
     for z in range(8):
         state[0, z + 1, pl.ds(8, 64), :] = scalar[z].astype(F32)
-        ysend[0, 0, pl.ds(z, 1), :] = state[0, z + 1, pl.ds(8, 1), :]
-        ysend[0, 1, pl.ds(z, 1), :] = state[0, z + 1, pl.ds(71, 1), :]
     zsend[0, 0] = scalar[0]
     zsend[0, 1] = scalar[7]
     for q in range(4):
         send_z(0, q)
     for side in range(2):
+        for z in range(8):
+            edge[pl.ds(z, 1), :] = state[0, z + 1, pl.ds(8 + 63 * side, 1), :]
+        pack_edge(0, side)
         send_y(0, side)
     for name in TABLES[1:]:
         loads[name].wait()
     loads["mask"].wait()
     spectral(0, first, first1)
-
-    def back_in_x(t, c):
-        arrived(rai.at[t, c], a_recv.at[2 * t + 1, c])
-        arrived(rui.at[t, c], u_recv.at[2 * t + 1, c])
-        x_inverse(t, c)
 
     def sent(t, c):
         for k in (2 * t, 2 * t + 1):
@@ -602,7 +653,7 @@
             sent_v(k, c)
 
     def middle(c):
-        back_in_x(0, c)
+        x_inverse(0, c)
         sent(0, c)
         x_forward(1, c)
         x_forward1(1, c)
@@ -622,7 +673,7 @@
         return c
 
     def last(c):
-        back_in_x(1, c)
+        x_inverse(1, c)
         pltpu.make_async_copy(field.at[c], velocity_h.at[c], out_sem.at[c]).start()
         lax.fori_loop(0, 8, coefficients, c)
         sent(1, c)
@@ -650,8 +701,11 @@
             if q in (0, 3):
                 side = q // 3
                 arrived(yrecv.at[s, side], y_rsem.at[s, side])
+                halo = yrecv[s, side].astype(F32)
                 for z in range(8):
-                    state[now, z + 1, pl.ds(7 + 65 * side, 1), :] = yrecv[s, side, pl.ds(z, 1), :]
+                    for half in range(2):
+                        lanes = slice(half * 256, half * 256 + 256)
+                        state[now, z + 1, pl.ds(7 + 65 * side, 1), lanes] = halo[8 * half + z : 8 * half + z + 1]
             for side in range(2):
                 arrived(zrecv.at[s, side, cells], z_rsem.at[s, side, q])
             bottom = block(1, q, zrecv[s, 0, cells].astype(F32), state[now, 2, rows])
@@ -671,7 +725,8 @@
                 @pl.when(s < SECTIONS - 1)
                 def _():
                     for z in range(8):
-                        ysend[s + 1, side, pl.ds(z, 1), :] = state[later, z + 1, pl.ds(8 + 63 * side, 1), :]
+                        edge[pl.ds(z, 1), :] = state[later, z + 1, pl.ds(8 + 63 * side, 1), :]
+                    pack_edge(s + 1, side)
                     send_y(s + 1, side)
         return carry
 
@@ -691,7 +746,11 @@
 
 
 def place_kernel(velocity_in, conc_in, velocity, conc, held, in_sem, out_sem):
-    pairs = [(velocity_in.at[c], held.at[c], velocity.at[c]) for c in range(3)] + [(conc_in, held.at[3], conc)]
+    pairs = []
+    for half in range(2):
+        planes = pl.ds(4 * half, 4)
+        pairs += [(velocity_in.at[c, planes], held.at[c, planes], velocity.at[c, planes]) for c in range(3)]
+        pairs.append((conc_in.at[planes], held.at[3, planes], conc.at[planes]))
     loads = [pltpu.make_async_copy(a, b, in_sem.at[i]) for i, (a, b, _) in enumerate(pairs)]
     stores = [pltpu.make_async_copy(b, c, out_sem.at[i]) for i, (_, b, c) in enumerate(pairs)]
     for copy in loads:
@@ -726,10 +785,11 @@
         vm((3, 2, 256, 256), BF), vm((2, 3, 16, 64, 128), BF),
         vm((3, 16, 64, 128), BF), vm((2, 3, 16, 64, 128), BF),
         vm((3, 512, 256), F32), vm((3, 512, 256), BF), vm((3, 512, 256), BF),
-        vm((512, 256), BF),
+        vm((512, 256), BF), vm((2, 256, 256), F32), vm((512, 256), F32),
+        vm((512, 512), F32),
         dma((4, 3)), dma((4, 3)), dma((4, 3)), dma((4, 3)),
         vm((SECTIONS, 2, 64, 512), BF), vm((SECTIONS, 2, 64, 512), BF),
-        vm((SECTIONS, 2, 8, 512), F32), vm((SECTIONS, 2, 8, 512), F32),
+        vm((SECTIONS, 2, 16, 256), BF), vm((SECTIONS, 2, 16, 256), BF), vm((8, 512), F32),
         vm((7, 8, 64, 512), F32), vm((2, 10, 80, 512), F32), vm((8, 64, 512), BF),
         dma((5,)), dma((len(TABLES),)),
         dma((4, 3)), dma((4, 3)), dma((4, 3)), dma((4, 3)),
@@ -764,7 +824,7 @@
         ),
         in_specs=[any_spec] * 2,
         out_specs=(any_spec, any_spec),
-        scratch_shapes=[vm((4, 8, 64, 512), BF), dma((4,)), dma((4,))],
+        scratch_shapes=[vm((4, 8, 64, 512), BF), dma((8,)), dma((8,))],
         name="place",
     )(velocity, conc)
 

time: 127 us -> 125 us (0.984)
  Pallas kernels: 126 us -> 124 us
    pallas_call x1, Pallas kernels: 123 us -> 122 us  [local(): pl.pallas_call(mixer_kernel, out_shape=(jax.ShapeDtypeStruct((3, 8, 64, 5...]
where the time goes in v4:
time: 125 us
  Pallas kernels  124 us (99%)
    pallas_call x1, Pallas kernels, local(): pl.pallas_call(mixer_kernel, out_shape=(jax.ShapeDtypeStruct((3, 8, 64, 5...  122 us

profile of v4, /device:TPU:0, one launch (start us, length us, event | category | flops | bytes accessed | tf_op | source)
XLA Modules:
  0.0 124.8 jit_solution(10639855625412861171)
XLA Ops:
  0.6 121.6 %mixer.1 = (bf16[3,8,64,512]{3,2,1,0:T(8,128)(2,1)}, bf16[8,64,512]{2,1,0:T(8,128)(2,1)}) custom-call(bf16[3,8,64,512]{3,2,1,0:T(8,128)(2,1)} %refs_0_.1, s32[8,64,512]{2,1,0:T(8,128)} %refs_1_.1, bf16[8,64,512]{2,1,0:T(8,128)(2,1)} %refs_2_.1, bf16[512,512]{1,0:T(8,128)(2,1)} %constant.24.clone.refs_3_, bf16[512,512]{1,0:T(8,128)(2,1)} %constant.25.clone.refs_4_, ...), custom_call_target="tpu_custom_call" | custom-call | tf_op jit(solution)/shard_map/mixer/pallas_call | solution.py:800
  122.2 2.4 %place.1 = (bf16[3,8,64,512]{3,2,1,0:T(8,128)(2,1)}, bf16[8,64,512]{2,1,0:T(8,128)(2,1)}) custom-call(bf16[3,8,64,512]{3,2,1,0:T(8,128)(2,1)} %get-tuple-element.4.velocity_in, bf16[8,64,512]{2,1,0:T(8,128)(2,1)} %get-tuple-element.5.conc_in), custom_call_target="tpu_custom_call" | custom-call | tf_op jit(solution)/shard_map/place/pallas_call | solution.py:819

commit v5 on v4

--- a/solution.py
+++ b/solution.py
@@ -155,7 +155,7 @@
     (field, mask, scalar, *rest) = refs[5 + count :]
     tab = dict(zip(TABLES, rest[:count]))
     (gain, inv, sa, ra, sb, rb, sbi, rbi, sai, rai, spec, first, second, lines, big, mid,
-     gain1, inv1, su, ru, sv, rv, svi, rvi, sui, rui, spec1, first1, second1, stacked, dots, dots1, summed,
+     gain1, inv1, su, ru, sv, rv, svi, rvi, sui, rui, spec1, first1, second1, stacked, dots, dots1, summed, big1,
      u_send, u_recv, v_send, v_recv,
      zsend, zrecv, ysend, yrecv, edge, coef, state, conc,
      in_sem, tab_sem, a_send, a_recv, b_send, b_recv, z_ssem, z_rsem, y_ssem, y_rsem, out_sem) = rest[count:]
@@ -225,11 +225,10 @@
             device_id=device, device_id_type=MESH)
 
     my_rows = pl.ds(pl.multiple_of(r * 64, 64), 64)
-    my_lanes = pl.ds(pl.multiple_of(xl * 128, 128), 128)
     my_slab = pl.ds(pl.multiple_of(e * 32, 32), 32)
 
     def send_a(t, i):
-        target = ra.at[t, i, :, my_rows, my_lanes]
+        target = ra.at[t, i, :, xl, my_rows]
         recv = a_recv.at[2 * t, i]
 
         for to, device in x_peers:
@@ -242,8 +241,7 @@
 
         def piece(to):
             rows = pl.ds(pl.multiple_of((to & 3) * 64, 64), 64)
-            lanes = pl.ds(pl.multiple_of((to // 4) * 128, 128), 128)
-            return sai.at[i, :, rows, lanes]
+            return sai.at[i, :, to // 4, rows]
 
         for to, device in x_peers:
             remote(piece(to), target, a_send.at[2 * t + 1, i], recv, device).start()
@@ -266,7 +264,7 @@
         pltpu.make_async_copy(source.at[c, e], target, recv).start()
 
     def send_v(t, c):
-        target = rv.at[t, c, :, my_rows, my_lanes]
+        target = rv.at[t, c, :, xl, my_rows]
         recv = v_recv.at[2 * t, c]
         for to, device in x_peers:
             remote(sv.at[c, pl.ds(2 * to, 2)], target, v_send.at[2 * t, c], recv, device).start()
@@ -278,8 +276,7 @@
 
         def piece(to):
             rows = pl.ds(pl.multiple_of((to & 3) * 64, 64), 64)
-            lanes = pl.ds(pl.multiple_of((to // 4) * 128, 128), 128)
-            return svi.at[c, :, rows, lanes]
+            return svi.at[c, :, to // 4, rows]
 
         for to, device in x_peers:
             remote(piece(to), target, v_send.at[2 * t + 1, c], recv, device).start()
@@ -366,16 +363,18 @@
 
     def y_forward(t, i):
         arrived(ra.at[t, i], a_recv.at[2 * t, i])
-        sb[i] = dot(tab["ty"][...], ra[t, i].reshape(512, 256)).astype(BF)
+        sides = [ra[t, i, :, side].reshape(512, 128) for side in range(2)]
+        sb[i] = dot(tab["ty"][...], jnp.concatenate(sides, axis=1)).astype(BF)
         send_b(sb, rb, 2 * t, t, i)
 
     def y_inverse(t, i):
         arrived(rbi.at[t, i], b_recv.at[2 * t + 1, i])
-        sai[i] = dot(tab["tyi"][...], rbi[t, i]).astype(BF).reshape(2, 256, 256)
+        out = dot(tab["tyi"][...], rbi[t, i]).astype(BF)
+        for side in range(2):
+            sai[i, :, side] = out[:, side * 128 : side * 128 + 128].reshape(2, 256, 128)
         send_ai(t, i)
 
     def z_forward(t, i):
-        arrived(rb.at[t, i], b_recv.at[2 * t, i])
         for half in range(2):
             lanes = slice(half * 128, half * 128 + 128)
 
@@ -461,17 +460,18 @@
         return dot(table, stacked[...]).astype(BF)
 
     def w_forward(t, c):
-        arrived(rv.at[t, c], v_recv.at[2 * t, c])
         for k1 in range(2):
-            values = rv[t, c, k1]
-            big[k1 * 256 : k1 * 256 + 256, :] = y_product(tab["uy"][...], values, values.astype(F32))
-        spec1[c] = dot(big[...], tab["uz"][...])
+            values = jnp.concatenate([rv[t, c, k1, 0], rv[t, c, k1, 1]], axis=1)
+            big1[k1 * 256 : k1 * 256 + 256, :] = y_product(tab["uy"][...], values, values.astype(F32))
+        spec1[c] = dot(big1[...], tab["uz"][...])
 
     def w_inverse(source, t, c):
         wide = dot(source[c], tab["uzi"][...])
         for k1 in range(2):
             part = wide[k1 * 256 : k1 * 256 + 256]
-            svi[c, k1] = y_product(tab["uyi"][...], part.astype(BF), part)
+            out = y_product(tab["uyi"][...], part.astype(BF), part)
+            for side in range(2):
+                svi[c, k1, side] = out[:, side * 128 : side * 128 + 128]
         send_vi(t, c)
 
     lane = lax.broadcasted_iota(jnp.int32, (16, 256), 1)
@@ -591,7 +591,12 @@
             y_forward(t, c)
             v_forward(t, c)
 
+        def inner_arrived(c):
+            arrived(rv.at[t, c], v_recv.at[2 * t, c])
+            arrived(rb.at[t, c], b_recv.at[2 * t, c])
+
         def inner(c):
+            inner_arrived(c)
             w_forward(t, c)
             z_forward(t, c)
 
@@ -607,10 +612,11 @@
         each(2, inner)
         parts1()
         parts()
+        inner_arrived(2)
         w_forward(t, 2)
+        z_forward(t, 2)
         project1_x(t)
         w_inverse(source1, t, 0)
-        z_forward(t, 2)
         project_x(t)
         z_inverse(source, t, 0)
         project1_yz(t)
@@ -773,20 +779,20 @@
         scratch.append(vm(shape, value.dtype))
     scratch += [
         vm((256, 256), F32), vm((256, 256), F32),
-        vm((3, 8, 2, 64, 128), BF), vm((2, 3, 2, 256, 256), BF),
+        vm((3, 8, 2, 64, 128), BF), vm((2, 3, 2, 2, 256, 128), BF),
         vm((3, 512, 256), BF), vm((2, 3, 512, 256), BF),
         vm((3, 512, 256), BF), vm((2, 3, 512, 256), BF),
-        vm((3, 2, 256, 256), BF), vm((2, 3, 8, 2, 64, 128), BF),
+        vm((3, 2, 2, 256, 128), BF), vm((2, 3, 8, 2, 64, 128), BF),
         vm((3, 2, 256, 256), F32), vm((3, 2, 256, 256), BF), vm((3, 2, 256, 256), BF),
         vm((512, 512), BF), vm((512, 256), BF), vm((4, 4, 2, 16, 256), F32),
         vm((512, 256), F32), vm((512, 256), F32),
         vm((3, 16, 64, 128), BF), vm((2, 3, 16, 64, 128), BF),
-        vm((3, 16, 64, 128), BF), vm((2, 3, 2, 256, 256), BF),
-        vm((3, 2, 256, 256), BF), vm((2, 3, 16, 64, 128), BF),
+        vm((3, 16, 64, 128), BF), vm((2, 3, 2, 2, 256, 128), BF),
+        vm((3, 2, 2, 256, 128), BF), vm((2, 3, 16, 64, 128), BF),
         vm((3, 16, 64, 128), BF), vm((2, 3, 16, 64, 128), BF),
         vm((3, 512, 256), F32), vm((3, 512, 256), BF), vm((3, 512, 256), BF),
         vm((512, 256), BF), vm((2, 256, 256), F32), vm((512, 256), F32),
-        vm((512, 512), F32),
+        vm((512, 512), F32), vm((512, 256), BF),
         dma((4, 3)), dma((4, 3)), dma((4, 3)), dma((4, 3)),
         vm((SECTIONS, 2, 64, 512), BF), vm((SECTIONS, 2, 64, 512), BF),
         vm((SECTIONS, 2, 16, 256), BF), vm((SECTIONS, 2, 16, 256), BF), vm((8, 512), F32),

time: 125 us -> 125 us (level)
  no operation moved by 1% of the time
where the time goes in v5:
time: 125 us
  Pallas kernels  124 us (99%)
    pallas_call x1, Pallas kernels, local(): pl.pallas_call(mixer_kernel, out_shape=(jax.ShapeDtypeStruct((3, 8, 64, 5...  122 us

profile of v5, /device:TPU:0, one launch (start us, length us, event | category | flops | bytes accessed | tf_op | source)
XLA Modules:
  0.0 124.9 jit_solution(9153291906030249897)
XLA Ops:
  0.6 121.8 %mixer.1 = (bf16[3,8,64,512]{3,2,1,0:T(8,128)(2,1)}, bf16[8,64,512]{2,1,0:T(8,128)(2,1)}) custom-call(bf16[3,8,64,512]{3,2,1,0:T(8,128)(2,1)} %refs_0_.1, s32[8,64,512]{2,1,0:T(8,128)} %refs_1_.1, bf16[8,64,512]{2,1,0:T(8,128)(2,1)} %refs_2_.1, bf16[512,512]{1,0:T(8,128)(2,1)} %constant.24.clone.refs_3_, bf16[512,512]{1,0:T(8,128)(2,1)} %constant.25.clone.refs_4_, ...), custom_call_target="tpu_custom_call" | custom-call | tf_op jit(solution)/shard_map/mixer/pallas_call | solution.py:806
  122.4 2.4 %place.1 = (bf16[3,8,64,512]{3,2,1,0:T(8,128)(2,1)}, bf16[8,64,512]{2,1,0:T(8,128)(2,1)}) custom-call(bf16[3,8,64,512]{3,2,1,0:T(8,128)(2,1)} %get-tuple-element.4.velocity_in, bf16[8,64,512]{2,1,0:T(8,128)(2,1)} %get-tuple-element.5.conc_in), custom_call_target="tpu_custom_call" | custom-call | tf_op jit(solution)/shard_map/place/pallas_call | solution.py:825

commit v6 on v5

--- a/solution.py
+++ b/solution.py
@@ -13,8 +13,8 @@
 F32 = jnp.float32
 TWO_PI = 2.0 * np.pi
 PLANE_ORDER = (
-    (1, 0), (3, 0), (0, 1), (0, 3), (1, 1), (3, 3), (1, 3), (3, 1),
-    (2, 0), (0, 2), (2, 1), (1, 2), (2, 3), (3, 2), (2, 2),
+    (2, 2), (2, 1), (1, 2), (2, 3), (3, 2), (2, 0), (0, 2), (1, 1), (3, 3), (1, 3), (3, 1),
+    (1, 0), (3, 0), (0, 1), (0, 3),
 )
 
 
@@ -202,12 +202,10 @@
 
     x_peers = [
         x_peer(step, core if same else 1 - core)
-        for step, same in ((1, 1), (3, 1), (1, 0), (3, 0), (2, 1), (2, 0), (0, 0))
+        for step, same in ((2, 1), (2, 0), (1, 1), (3, 1), (1, 0), (3, 0), (0, 0))
     ]
     plane_peers = [plane_peer(dy, dz) for dy, dz in PLANE_ORDER]
 
-    z_up = (r, lax.rem(col + 1, 32))
-    z_down = (r, lax.rem(col + 31, 32))
     y_up = (lax.rem(r + 1, 4), col)
     y_down = (lax.rem(r + 3, 4), col)
 
@@ -297,11 +295,12 @@
     def sent_v(k, i):
         arrived(sv.at[i, pl.ds(0, 14)], v_send.at[k, i])
 
-    def send_z(s, q):
+    near, far = 1 - xl, xl
+
+    def send_z(s, side, q):
         rows = pl.ds(16 * q, 16)
-        for side, device in ((0, z_down), (1, z_up)):
-            remote(zsend.at[s, side, rows], zrecv.at[s, 1 - side, rows],
-                   z_ssem.at[s, side], z_rsem.at[s, 1 - side, q], device).start()
+        remote(zsend.at[s, side, rows], zrecv.at[s, 1 - side, rows], z_ssem.at[s, side],
+               z_rsem.at[s, 1 - side, q], (r, (col + 2 * side + 31) & 31)).start()
 
     def pack_edge(s, side):
         value = edge[...]
@@ -639,8 +638,9 @@
         state[0, z + 1, pl.ds(8, 64), :] = scalar[z].astype(F32)
     zsend[0, 0] = scalar[0]
     zsend[0, 1] = scalar[7]
-    for q in range(4):
-        send_z(0, q)
+    for side in (far, near):
+        for q in range(4):
+            send_z(0, side, q)
     for side in range(2):
         for z in range(8):
             edge[pl.ds(z, 1), :] = state[0, z + 1, pl.ds(8 + 63 * side, 1), :]
@@ -689,7 +689,7 @@
     def section(s, carry):
         now, later = s & 1, (s + 1) & 1
 
-        def block(z, q, below_z, above_z):
+        def block(z, q):
             at = 8 + 16 * q
             rows, cells = pl.ds(at, 16), pl.ds(16 * q, 16)
             center = state[now, z, rows]
@@ -698,12 +698,23 @@
             new = new + coef[1, z - 1, cells] * pltpu.roll(center, 511, 1)
             new = new + coef[2, z - 1, cells] * state[now, z, pl.ds(at - 1, 16)]
             new = new + coef[3, z - 1, cells] * state[now, z, pl.ds(at + 1, 16)]
-            new = new + coef[4, z - 1, cells] * below_z + coef[5, z - 1, cells] * above_z
+            new = new + coef[4, z - 1, cells] * state[now, z - 1, rows]
+            new = new + coef[5, z - 1, cells] * state[now, z + 1, rows]
             state[later, z, rows] = new
             return new
 
+        def outer_block(side, q):
+            cells = pl.ds(16 * q, 16)
+            arrived(zrecv.at[s, side, cells], z_rsem.at[s, side, q])
+            state[now, 9 * side, pl.ds(8 + 16 * q, 16)] = zrecv[s, side, cells].astype(F32)
+            face = block(1 + 7 * side, q)
+
+            @pl.when(s < SECTIONS - 1)
+            def _():
+                zsend[s + 1, side, cells] = face.astype(BF)
+                send_z(s + 1, side, q)
+
         for q in (1, 2, 0, 3):
-            rows, cells = pl.ds(8 + 16 * q, 16), pl.ds(16 * q, 16)
             if q in (0, 3):
                 side = q // 3
                 arrived(yrecv.at[s, side], y_rsem.at[s, side])
@@ -712,19 +723,12 @@
                     for half in range(2):
                         lanes = slice(half * 256, half * 256 + 256)
                         state[now, z + 1, pl.ds(7 + 65 * side, 1), lanes] = halo[8 * half + z : 8 * half + z + 1]
-            for side in range(2):
-                arrived(zrecv.at[s, side, cells], z_rsem.at[s, side, q])
-            bottom = block(1, q, zrecv[s, 0, cells].astype(F32), state[now, 2, rows])
-            top = block(8, q, state[now, 7, rows], zrecv[s, 1, cells].astype(F32))
-
-            @pl.when(s < SECTIONS - 1)
-            def _():
-                zsend[s + 1, 0, cells] = bottom.astype(BF)
-                zsend[s + 1, 1, cells] = top.astype(BF)
-                send_z(s + 1, q)
-
+            outer_block(near, q)
             for z in range(2, 8):
-                block(z, q, state[now, z - 1, rows], state[now, z + 1, rows])
+                block(z, q)
+
+        for q in (0, 3, 1, 2):
+            outer_block(far, q)
             if q in (0, 3):
                 side = q // 3
 

time: 125 us -> 124 us (level)
    pallas_call x1, Pallas kernels: 122 us -> 120 us  [local(): pl.pallas_call(mixer_kernel, out_shape=(jax.ShapeDtypeStruct((3, 8, 64, 5...]
where the time goes in v6:
time: 124 us
  Pallas kernels  123 us (99%)
    pallas_call x1, Pallas kernels, local(): pl.pallas_call(mixer_kernel, out_shape=(jax.ShapeDtypeStruct((3, 8, 64, 5...  120 us

profile of v6, /device:TPU:0, one launch (start us, length us, event | category | flops | bytes accessed | tf_op | source)
XLA Modules:
  0.0 123.6 jit_solution(14536413977987088446)
XLA Ops:
  0.6 120.5 %mixer.1 = (bf16[3,8,64,512]{3,2,1,0:T(8,128)(2,1)}, bf16[8,64,512]{2,1,0:T(8,128)(2,1)}) custom-call(bf16[3,8,64,512]{3,2,1,0:T(8,128)(2,1)} %refs_0_.1, s32[8,64,512]{2,1,0:T(8,128)} %refs_1_.1, bf16[8,64,512]{2,1,0:T(8,128)(2,1)} %refs_2_.1, bf16[512,512]{1,0:T(8,128)(2,1)} %constant.24.clone.refs_3_, bf16[512,512]{1,0:T(8,128)(2,1)} %constant.25.clone.refs_4_, ...), custom_call_target="tpu_custom_call" | custom-call | tf_op jit(solution)/shard_map/mixer/pallas_call | solution.py:810
  121.1 2.4 %place.1 = (bf16[3,8,64,512]{3,2,1,0:T(8,128)(2,1)}, bf16[8,64,512]{2,1,0:T(8,128)(2,1)}) custom-call(bf16[3,8,64,512]{3,2,1,0:T(8,128)(2,1)} %get-tuple-element.4.velocity_in, bf16[8,64,512]{2,1,0:T(8,128)(2,1)} %get-tuple-element.5.conc_in), custom_call_target="tpu_custom_call" | custom-call | tf_op jit(solution)/shard_map/place/pallas_call | solution.py:829

commit v7 on v6

--- a/solution.py
+++ b/solution.py
@@ -179,12 +179,14 @@
         return load(source, tab[name], sem)
 
     loads = {0: load(force_h.at[0], field.at[0], in_sem.at[0]), "fx": load_table("fx")}
-    for i in (1, 2):
-        loads[i] = load(force_h.at[i], field.at[i], in_sem.at[i])
-    loads["scalar"] = load(scalar_h, scalar, in_sem.at[4])
-    for name in TABLES[1:]:
-        loads[name] = load_table(name)
-    loads["mask"] = load(mask_h, mask, in_sem.at[3])
+
+    def load_rest():
+        for i in (1, 2):
+            loads[i] = load(force_h.at[i], field.at[i], in_sem.at[i])
+        for name in TABLES[1:]:
+            loads[name] = load_table(name)
+        loads["scalar"] = load(scalar_h, scalar, in_sem.at[4])
+        loads["mask"] = load(mask_h, mask, in_sem.at[3])
 
     core = r & 1
     x = (r // 2) * 2 + xl
@@ -623,13 +625,17 @@
         each(2, outer)
         each(3, back)
 
-    loads["fx"].wait()
-    for i in range(3):
-        loads[i].wait()
     def start(c):
+        @pl.when(c > 0)
+        def _():
+            arrived(field.at[c], in_sem.at[c])
+
         x_forward(0, c)
         x_forward1(0, c)
 
+    loads["fx"].wait()
+    loads[0].wait()
+    load_rest()
     each(3, start)
     lax.fori_loop(0, 16, factors, 0)
     lax.fori_loop(0, 32, factors1, 0)
@@ -681,78 +687,106 @@
     def last(c):
         x_inverse(1, c)
         pltpu.make_async_copy(field.at[c], velocity_h.at[c], out_sem.at[c]).start()
-        lax.fori_loop(0, 8, coefficients, c)
-        sent(1, c)
+
+        @pl.when(c < 2)
+        def _():
+            lax.fori_loop(0, 8, coefficients, c)
 
     each(3, last)
 
+    def block(s, z, q):
+        now, later = s & 1, (s + 1) & 1
+        at = 8 + 16 * q
+        rows, cells = pl.ds(at, 16), pl.ds(16 * q, 16)
+        center = state[now, z, rows]
+        new = coef[6, z - 1, cells] * center
+        new = new + coef[0, z - 1, cells] * pltpu.roll(center, 1, 1)
+        new = new + coef[1, z - 1, cells] * pltpu.roll(center, 511, 1)
+        new = new + coef[2, z - 1, cells] * state[now, z, pl.ds(at - 1, 16)]
+        new = new + coef[3, z - 1, cells] * state[now, z, pl.ds(at + 1, 16)]
+        new = new + coef[4, z - 1, cells] * state[now, z - 1, rows]
+        new = new + coef[5, z - 1, cells] * state[now, z + 1, rows]
+        state[later, z, rows] = new
+        return new
+
+    def outer_block(s, side, q):
+        cells = pl.ds(16 * q, 16)
+        arrived(zrecv.at[s, side, cells], z_rsem.at[s, side, q])
+        state[s & 1, 9 * side, pl.ds(8 + 16 * q, 16)] = zrecv[s, side, cells].astype(F32)
+        face = block(s, 1 + 7 * side, q)
+
+        @pl.when(s < SECTIONS - 1)
+        def _():
+            zsend[s + 1, side, cells] = face.astype(BF)
+            send_z(s + 1, side, q)
+
+    def y_halo(s):
+        for side in range(2):
+            arrived(yrecv.at[s, side], y_rsem.at[s, side])
+            halo = yrecv[s, side].astype(F32)
+            for z in range(8):
+                for half in range(2):
+                    lanes = slice(half * 256, half * 256 + 256)
+                    state[s & 1, z + 1, pl.ds(7 + 65 * side, 1), lanes] = halo[8 * half + z : 8 * half + z + 1]
+
     def section(s, carry):
-        now, later = s & 1, (s + 1) & 1
-
-        def block(z, q):
-            at = 8 + 16 * q
-            rows, cells = pl.ds(at, 16), pl.ds(16 * q, 16)
-            center = state[now, z, rows]
-            new = coef[6, z - 1, cells] * center
-            new = new + coef[0, z - 1, cells] * pltpu.roll(center, 1, 1)
-            new = new + coef[1, z - 1, cells] * pltpu.roll(center, 511, 1)
-            new = new + coef[2, z - 1, cells] * state[now, z, pl.ds(at - 1, 16)]
-            new = new + coef[3, z - 1, cells] * state[now, z, pl.ds(at + 1, 16)]
-            new = new + coef[4, z - 1, cells] * state[now, z - 1, rows]
-            new = new + coef[5, z - 1, cells] * state[now, z + 1, rows]
-            state[later, z, rows] = new
-            return new
-
-        def outer_block(side, q):
-            cells = pl.ds(16 * q, 16)
-            arrived(zrecv.at[s, side, cells], z_rsem.at[s, side, q])
-            state[now, 9 * side, pl.ds(8 + 16 * q, 16)] = zrecv[s, side, cells].astype(F32)
-            face = block(1 + 7 * side, q)
-
-            @pl.when(s < SECTIONS - 1)
-            def _():
-                zsend[s + 1, side, cells] = face.astype(BF)
-                send_z(s + 1, side, q)
-
-        for q in (1, 2, 0, 3):
-            if q in (0, 3):
-                side = q // 3
-                arrived(yrecv.at[s, side], y_rsem.at[s, side])
-                halo = yrecv[s, side].astype(F32)
-                for z in range(8):
-                    for half in range(2):
-                        lanes = slice(half * 256, half * 256 + 256)
-                        state[now, z + 1, pl.ds(7 + 65 * side, 1), lanes] = halo[8 * half + z : 8 * half + z + 1]
-            outer_block(near, q)
+        @pl.when(s == SECTIONS - 1)
+        def _():
+            y_halo(s)
+
+        for q in (0, 3, 1, 2):
+            outer_block(s, near, q)
             for z in range(2, 8):
-                block(z, q)
-
-        for q in (0, 3, 1, 2):
-            outer_block(far, q)
+                block(s, z, q)
             if q in (0, 3):
                 side = q // 3
 
                 @pl.when(s < SECTIONS - 1)
                 def _():
                     for z in range(8):
-                        edge[pl.ds(z, 1), :] = state[later, z + 1, pl.ds(8 + 63 * side, 1), :]
+                        edge[pl.ds(z, 1), :] = state[(s + 1) & 1, z + 1, pl.ds(8 + 63 * side, 1), :]
                     pack_edge(s + 1, side)
                     send_y(s + 1, side)
+
+        following = jnp.minimum(s + 1, SECTIONS - 1)
+
+        @pl.when(s != SECTIONS - 2)
+        def _():
+            for q in (1, 2):
+                outer_block(following, far, q)
+
+        @pl.when(s < SECTIONS - 2)
+        def _():
+            y_halo(s + 1)
+
+        @pl.when(s != SECTIONS - 2)
+        def _():
+            for q in (0, 3):
+                outer_block(following, far, q)
+
         return carry
 
+    y_halo(0)
+    coefficients(7 * far, 2)
+    for q in (1, 2, 0, 3):
+        outer_block(0, far, q)
+    lax.fori_loop(0, 7, lambda n, carry: coefficients(n + near, carry), 2)
     lax.fori_loop(0, SECTIONS, section, 0)
-    for z in range(8):
-        conc[z] = state[SECTIONS % 2, z + 1, pl.ds(8, 64), :].astype(BF)
-
+    for half in range(2):
+        planes = pl.ds(4 * half, 4)
+        conc[planes] = state[SECTIONS % 2, pl.ds(1 + 4 * half, 4), pl.ds(8, 64), :].astype(BF)
+        pltpu.make_async_copy(conc.at[planes], conc_h.at[planes], out_sem.at[3 + half]).start()
+
+    each(3, lambda c: sent(1, c))
     for s in range(SECTIONS):
         for i in range(2):
             arrived(zsend.at[s, i], z_ssem.at[s, i])
             arrived(ysend.at[s, i], y_ssem.at[s, i])
-    out = pltpu.make_async_copy(conc, conc_h, out_sem.at[3])
-    out.start()
     for c in range(3):
         pltpu.make_async_copy(field.at[c], velocity_h.at[c], out_sem.at[c]).wait()
-    out.wait()
+    for half in range(2):
+        planes = pl.ds(4 * half, 4)
+        pltpu.make_async_copy(conc.at[planes], conc_h.at[planes], out_sem.at[3 + half]).wait()
 
 
 def place_kernel(velocity_in, conc_in, velocity, conc, held, in_sem, out_sem):
@@ -804,7 +838,7 @@
         dma((5,)), dma((len(TABLES),)),
         dma((4, 3)), dma((4, 3)), dma((4, 3)), dma((4, 3)),
         dma((SECTIONS, 2)), dma((SECTIONS, 2, 4)), dma((SECTIONS, 2)), dma((SECTIONS, 2)),
-        dma((4,)),
+        dma((5,)),
     ]
     any_spec = pl.BlockSpec(memory_space=pl.ANY)
     velocity, conc = pl.pallas_call(

time: 124 us -> 123 us (level)
  Pallas kernels: 123 us -> 121 us
    pallas_call x1, Pallas kernels: 120 us -> 118 us  [local(): pl.pallas_call(mixer_kernel, out_shape=(jax.ShapeDtypeStruct((3, 8, 64, 5...]
where the time goes in v7:
time: 123 us; the launch traced here: 122 us
  Pallas kernels  121 us (98%)
    pallas_call x1, Pallas kernels, local(): pl.pallas_call(mixer_kernel, out_shape=(jax.ShapeDtypeStruct((3, 8, 64, 5...  118 us

profile of v7, /device:TPU:0, one launch (start us, length us, event | category | flops | bytes accessed | tf_op | source)
XLA Modules:
  0.0 121.5 jit_solution(17408402616132757204)
XLA Ops:
  0.6 118.3 %mixer.1 = (bf16[3,8,64,512]{3,2,1,0:T(8,128)(2,1)}, bf16[8,64,512]{2,1,0:T(8,128)(2,1)}) custom-call(bf16[3,8,64,512]{3,2,1,0:T(8,128)(2,1)} %refs_0_.1, s32[8,64,512]{2,1,0:T(8,128)} %refs_1_.1, bf16[8,64,512]{2,1,0:T(8,128)(2,1)} %refs_2_.1, bf16[512,512]{1,0:T(8,128)(2,1)} %constant.24.clone.refs_3_, bf16[512,512]{1,0:T(8,128)(2,1)} %constant.25.clone.refs_4_, ...), custom_call_target="tpu_custom_call" | custom-call | tf_op jit(solution)/shard_map/mixer/pallas_call | solution.py:844
  119.0 2.4 %place.1 = (bf16[3,8,64,512]{3,2,1,0:T(8,128)(2,1)}, bf16[8,64,512]{2,1,0:T(8,128)(2,1)}) custom-call(bf16[3,8,64,512]{3,2,1,0:T(8,128)(2,1)} %get-tuple-element.4.velocity_in, bf16[8,64,512]{2,1,0:T(8,128)(2,1)} %get-tuple-element.5.conc_in), custom_call_target="tpu_custom_call" | custom-call | tf_op jit(solution)/shard_map/place/pallas_call | solution.py:863

commit v8 on v7

--- a/solution.py
+++ b/solution.py
@@ -729,6 +729,10 @@
                     lanes = slice(half * 256, half * 256 + 256)
                     state[s & 1, z + 1, pl.ds(7 + 65 * side, 1), lanes] = halo[8 * half + z : 8 * half + z + 1]
 
+    def store_planes(z, count):
+        planes = pl.ds(z, count)
+        return pltpu.make_async_copy(conc.at[planes], conc_h.at[planes], out_sem.at[3 + (0, 1, 0, 0, 0, 0, 0, 2)[z]])
+
     def section(s, carry):
         @pl.when(s == SECTIONS - 1)
         def _():
@@ -748,6 +752,11 @@
                     pack_edge(s + 1, side)
                     send_y(s + 1, side)
 
+        @pl.when(s == SECTIONS - 1)
+        def _():
+            conc[pl.ds(1, 6)] = state[SECTIONS % 2, pl.ds(2, 6), pl.ds(8, 64), :].astype(BF)
+            store_planes(1, 6).start()
+
         following = jnp.minimum(s + 1, SECTIONS - 1)
 
         @pl.when(s != SECTIONS - 2)
@@ -772,10 +781,9 @@
         outer_block(0, far, q)
     lax.fori_loop(0, 7, lambda n, carry: coefficients(n + near, carry), 2)
     lax.fori_loop(0, SECTIONS, section, 0)
-    for half in range(2):
-        planes = pl.ds(4 * half, 4)
-        conc[planes] = state[SECTIONS % 2, pl.ds(1 + 4 * half, 4), pl.ds(8, 64), :].astype(BF)
-        pltpu.make_async_copy(conc.at[planes], conc_h.at[planes], out_sem.at[3 + half]).start()
+    for z in (0, 7):
+        conc[z] = state[SECTIONS % 2, z + 1, pl.ds(8, 64), :].astype(BF)
+        store_planes(z, 1).start()
 
     each(3, lambda c: sent(1, c))
     for s in range(SECTIONS):
@@ -784,9 +792,8 @@
             arrived(ysend.at[s, i], y_ssem.at[s, i])
     for c in range(3):
         pltpu.make_async_copy(field.at[c], velocity_h.at[c], out_sem.at[c]).wait()
-    for half in range(2):
-        planes = pl.ds(4 * half, 4)
-        pltpu.make_async_copy(conc.at[planes], conc_h.at[planes], out_sem.at[3 + half]).wait()
+    for z, count in ((0, 1), (1, 6), (7, 1)):
+        store_planes(z, count).wait()
 
 
 def place_kernel(velocity_in, conc_in, velocity, conc, held, in_sem, out_sem):
@@ -838,7 +845,7 @@
         dma((5,)), dma((len(TABLES),)),
         dma((4, 3)), dma((4, 3)), dma((4, 3)), dma((4, 3)),
         dma((SECTIONS, 2)), dma((SECTIONS, 2, 4)), dma((SECTIONS, 2)), dma((SECTIONS, 2)),
-        dma((5,)),
+        dma((6,)),
     ]
     any_spec = pl.BlockSpec(memory_space=pl.ANY)
     velocity, conc = pl.pallas_call(
@@ -851,7 +858,7 @@
         out_specs=(any_spec, any_spec),
         scratch_shapes=scratch,
         compiler_params=pltpu.CompilerParams(
-            collective_id=0, has_side_effects=True, vmem_limit_bytes=62 * 1024 * 1024
+            collective_id=0, has_side_effects=True, vmem_limit_bytes=52 * 1024 * 1024
         ),
         name="mixer",
     )(

time: 123 us -> 128 us (1.041)
  local copies, waits for them, and re-layouts: 0 us -> 4.57 us
    unnamed x0 -> x10, local copies, waits for them, and re-layouts: none -> 4.57 us
where the time goes in v8:
time: 128 us; the launch traced here: 125 us
  Pallas kernels  120 us (94%)
  local copies, waits for them, and re-layouts  4.57 us (4%)
    pallas_call x1, Pallas kernels, local(): pl.pallas_call(mixer_kernel, out_shape=(jax.ShapeDtypeStruct((3, 8, 64, 5...  118 us
    unnamed x10, local copies, waits for them, and re-layouts  4.57 us

profile of v8, /device:TPU:0, one launch (start us, length us, event | category | flops | bytes accessed | tf_op | source)
XLA Modules:
  0.0 125.5 jit_solution(7239137083795938747)
XLA Ops:
  0.6 0.0 copy-start.1
  0.6 0.9 copy-done.1
  1.6 0.0 copy-start.2
  1.6 0.9 copy-done.2
  2.5 0.0 copy-start.3
  2.5 0.9 copy-done.3
  3.5 0.0 copy-start.4
  3.5 0.9 copy-done.4
  4.4 117.7 %mixer.1 = (bf16[3,8,64,512]{3,2,1,0:T(8,128)(2,1)}, bf16[8,64,512]{2,1,0:T(8,128)(2,1)S(1)}) custom-call(bf16[3,8,64,512]{3,2,1,0:T(8,128)(2,1)} %refs_0_.1, s32[8,64,512]{2,1,0:T(8,128)} %refs_1_.1, bf16[8,64,512]{2,1,0:T(8,128)(2,1)} %refs_2_.1, bf16[512,512]{1,0:T(8,128)(2,1)} %constant.24.clone.refs_3_, bf16[512,512]{1,0:T(8,128)(2,1)} %constant.25.clone.refs_4_, ...), custom_call_target="tpu_custom_call" | custom-call | tf_op jit(solution)/shard_map/mixer/pallas_call | solution.py:851
  122.1 0.0 copy-start
  122.2 0.8 copy-done
  122.9 2.4 %place.1 = (bf16[3,8,64,512]{3,2,1,0:T(8,128)(2,1)}, bf16[8,64,512]{2,1,0:T(8,128)(2,1)}) custom-call(bf16[3,8,64,512]{3,2,1,0:T(8,128)(2,1)} %get-tuple-element.4.velocity_in, bf16[8,64,512]{2,1,0:T(8,128)(2,1)} %copy-done), custom_call_target="tpu_custom_call" | custom-call | tf_op jit(solution)/shard_map/place/pallas_call | solution.py:870
Async XLA Ops:
  0.6 1.0 copy-start.1
  1.6 0.9 copy-start.2
  2.5 0.9 copy-start.3
  3.5 0.9 copy-start.4
  122.1 0.8 copy-start

commit v9 on v8

--- a/solution.py
+++ b/solution.py
@@ -376,6 +376,7 @@
         send_ai(t, i)
 
     def z_forward(t, i):
+        arrived(rb.at[t, i], b_recv.at[2 * t, i])
         for half in range(2):
             lanes = slice(half * 128, half * 128 + 128)
 
@@ -461,6 +462,7 @@
         return dot(table, stacked[...]).astype(BF)
 
     def w_forward(t, c):
+        arrived(rv.at[t, c], v_recv.at[2 * t, c])
         for k1 in range(2):
             values = jnp.concatenate([rv[t, c, k1, 0], rv[t, c, k1, 1]], axis=1)
             big1[k1 * 256 : k1 * 256 + 256, :] = y_product(tab["uy"][...], values, values.astype(F32))
@@ -592,12 +594,7 @@
             y_forward(t, c)
             v_forward(t, c)
 
-        def inner_arrived(c):
-            arrived(rv.at[t, c], v_recv.at[2 * t, c])
-            arrived(rb.at[t, c], b_recv.at[2 * t, c])
-
         def inner(c):
-            inner_arrived(c)
             w_forward(t, c)
             z_forward(t, c)
 
@@ -613,11 +610,10 @@
         each(2, inner)
         parts1()
         parts()
-        inner_arrived(2)
         w_forward(t, 2)
-        z_forward(t, 2)
         project1_x(t)
         w_inverse(source1, t, 0)
+        z_forward(t, 2)
         project_x(t)
         z_inverse(source, t, 0)
         project1_yz(t)
@@ -858,7 +854,7 @@
         out_specs=(any_spec, any_spec),
         scratch_shapes=scratch,
         compiler_params=pltpu.CompilerParams(
-            collective_id=0, has_side_effects=True, vmem_limit_bytes=52 * 1024 * 1024
+            collective_id=0, has_side_effects=True, vmem_limit_bytes=62 * 1024 * 1024
         ),
         name="mixer",
     )(

time: 128 us -> 122 us (0.953)
  local copies, waits for them, and re-layouts: 4.57 us -> 0 us
    unnamed x10 -> x0, local copies, waits for them, and re-layouts: 4.57 us -> none
where the time goes in v9:
time: 122 us; the launch traced here: 120 us
  Pallas kernels  120 us (98%)
    pallas_call x1, Pallas kernels, local(): pl.pallas_call(mixer_kernel, out_shape=(jax.ShapeDtypeStruct((3, 8, 64, 5...  117 us

profile of v9, /device:TPU:0, one launch (start us, length us, event | category | flops | bytes accessed | tf_op | source)
XLA Modules:
  0.0 120.4 jit_solution(8122299088783691250)
XLA Ops:
  0.6 117.2 %mixer.1 = (bf16[3,8,64,512]{3,2,1,0:T(8,128)(2,1)}, bf16[8,64,512]{2,1,0:T(8,128)(2,1)}) custom-call(bf16[3,8,64,512]{3,2,1,0:T(8,128)(2,1)} %refs_0_.1, s32[8,64,512]{2,1,0:T(8,128)} %refs_1_.1, bf16[8,64,512]{2,1,0:T(8,128)(2,1)} %refs_2_.1, bf16[512,512]{1,0:T(8,128)(2,1)} %constant.24.clone.refs_3_, bf16[512,512]{1,0:T(8,128)(2,1)} %constant.25.clone.refs_4_, ...), custom_call_target="tpu_custom_call" | custom-call | tf_op jit(solution)/shard_map/mixer/pallas_call | solution.py:847
  117.9 2.4 %place.1 = (bf16[3,8,64,512]{3,2,1,0:T(8,128)(2,1)}, bf16[8,64,512]{2,1,0:T(8,128)(2,1)}) custom-call(bf16[3,8,64,512]{3,2,1,0:T(8,128)(2,1)} %get-tuple-element.4.velocity_in, bf16[8,64,512]{2,1,0:T(8,128)(2,1)} %get-tuple-element.5.conc_in), custom_call_target="tpu_custom_call" | custom-call | tf_op jit(solution)/shard_map/place/pallas_call | solution.py:866

commit v10 on v9

--- a/solution.py
+++ b/solution.py
@@ -178,7 +178,11 @@
             source = source.at[d if name in BY_D else (e & 7) + (8 * xl if name == "utw" else 0)]
         return load(source, tab[name], sem)
 
-    loads = {0: load(force_h.at[0], field.at[0], in_sem.at[0]), "fx": load_table("fx")}
+    for i in range(4):
+        planes, rows = pl.ds(2 * i, 2), pl.ds(128 * i, 128)
+        load(force_h.at[0, planes], field.at[0, planes], in_sem.at[0])
+        load(tables_h["fx"].at[rows], tab["fx"].at[rows], tab_sem.at[0])
+    loads = {}
 
     def load_rest():
         for i in (1, 2):
@@ -461,8 +465,15 @@
         stacked[0:256, :] = values
         return dot(table, stacked[...]).astype(BF)
 
-    def w_forward(t, c):
+    def first_faces(t):
+        for q in range(4):
+            send_z(0, near if t else far, q)
+        send_y(0, t)
+
+    def w_forward(t, c, last=False):
         arrived(rv.at[t, c], v_recv.at[2 * t, c])
+        if last:
+            first_faces(t)
         for k1 in range(2):
             values = jnp.concatenate([rv[t, c, k1, 0], rv[t, c, k1, 1]], axis=1)
             big1[k1 * 256 : k1 * 256 + 256, :] = y_product(tab["uy"][...], values, values.astype(F32))
@@ -610,7 +621,7 @@
         each(2, inner)
         parts1()
         parts()
-        w_forward(t, 2)
+        w_forward(t, 2, True)
         project1_x(t)
         w_inverse(source1, t, 0)
         z_forward(t, 2)
@@ -629,8 +640,8 @@
         x_forward(0, c)
         x_forward1(0, c)
 
-    loads["fx"].wait()
-    loads[0].wait()
+    arrived(tab["fx"], tab_sem.at[0])
+    arrived(field.at[0], in_sem.at[0])
     load_rest()
     each(3, start)
     lax.fori_loop(0, 16, factors, 0)
@@ -640,14 +651,10 @@
         state[0, z + 1, pl.ds(8, 64), :] = scalar[z].astype(F32)
     zsend[0, 0] = scalar[0]
     zsend[0, 1] = scalar[7]
-    for side in (far, near):
-        for q in range(4):
-            send_z(0, side, q)
     for side in range(2):
         for z in range(8):
             edge[pl.ds(z, 1), :] = state[0, z + 1, pl.ds(8 + 63 * side, 1), :]
         pack_edge(0, side)
-        send_y(0, side)
     for name in TABLES[1:]:
         loads[name].wait()
     loads["mask"].wait()

time: 122 us -> 119 us (0.975)
  Pallas kernels: 120 us -> 116 us
    pallas_call x1, Pallas kernels: 117 us -> 114 us  [local(): pl.pallas_call(mixer_kernel, out_shape=(jax.ShapeDtypeStruct((3, 8, 64, 5...]
where the time goes in v10:
time: 119 us; the launch traced here: 117 us
  Pallas kernels  116 us (97%)
    pallas_call x1, Pallas kernels, local(): pl.pallas_call(mixer_kernel, out_shape=(jax.ShapeDtypeStruct((3, 8, 64, 5...  114 us
    pallas_call x1, Pallas kernels, local(): pl.pallas_call(place_kernel, out_shape=(jax.ShapeDtypeStruct((3, 8, 64, 5...  2.4 us

profile of v10, /device:TPU:0, one launch (start us, length us, event | category | flops | bytes accessed | tf_op | source)
XLA Modules:
  0.0 117.0 jit_solution(1619049548520510588)
XLA Ops:
  0.6 113.9 %mixer.1 = (bf16[3,8,64,512]{3,2,1,0:T(8,128)(2,1)}, bf16[8,64,512]{2,1,0:T(8,128)(2,1)}) custom-call(bf16[3,8,64,512]{3,2,1,0:T(8,128)(2,1)} %refs_0_.1, s32[8,64,512]{2,1,0:T(8,128)} %refs_1_.1, bf16[8,64,512]{2,1,0:T(8,128)(2,1)} %refs_2_.1, bf16[512,512]{1,0:T(8,128)(2,1)} %constant.24.clone.refs_3_, bf16[512,512]{1,0:T(8,128)(2,1)} %constant.25.clone.refs_4_, ...), custom_call_target="tpu_custom_call" | custom-call | tf_op jit(solution)/shard_map/mixer/pallas_call | solution.py:854
  114.5 2.4 %place.1 = (bf16[3,8,64,512]{3,2,1,0:T(8,128)(2,1)}, bf16[8,64,512]{2,1,0:T(8,128)(2,1)}) custom-call(bf16[3,8,64,512]{3,2,1,0:T(8,128)(2,1)} %get-tuple-element.4.velocity_in, bf16[8,64,512]{2,1,0:T(8,128)(2,1)} %get-tuple-element.5.conc_in), custom_call_target="tpu_custom_call" | custom-call | tf_op jit(solution)/shard_map/place/pallas_call | solution.py:873

commit v11 on v10

--- a/solution.py
+++ b/solution.py
@@ -727,10 +727,9 @@
         for side in range(2):
             arrived(yrecv.at[s, side], y_rsem.at[s, side])
             halo = yrecv[s, side].astype(F32)
-            for z in range(8):
-                for half in range(2):
-                    lanes = slice(half * 256, half * 256 + 256)
-                    state[s & 1, z + 1, pl.ds(7 + 65 * side, 1), lanes] = halo[8 * half + z : 8 * half + z + 1]
+            for half in range(2):
+                lanes = slice(half * 256, half * 256 + 256)
+                state[s & 1, 1:9, 7 + 65 * side, lanes] = halo[8 * half : 8 * half + 8]
 
     def store_planes(z, count):
         planes = pl.ds(z, count)
@@ -750,8 +749,7 @@
 
                 @pl.when(s < SECTIONS - 1)
                 def _():
-                    for z in range(8):
-                        edge[pl.ds(z, 1), :] = state[(s + 1) & 1, z + 1, pl.ds(8 + 63 * side, 1), :]
+                    edge[...] = state[(s + 1) & 1, 1:9, 8 + 63 * side, :]
                     pack_edge(s + 1, side)
                     send_y(s + 1, side)
 

time: 119 us -> 120 us (level)
  no operation moved by 1% of the time
where the time goes in v11:
time: 120 us; the launch traced here: 117 us
  Pallas kernels  116 us (97%)
    pallas_call x1, Pallas kernels, local(): pl.pallas_call(mixer_kernel, out_shape=(jax.ShapeDtypeStruct((3, 8, 64, 5...  114 us

profile of v11, /device:TPU:0, one launch (start us, length us, event | category | flops | bytes accessed | tf_op | source)
XLA Modules:
  0.0 117.2 jit_solution(12049742878671465781)
XLA Ops:
  0.6 114.0 %mixer.1 = (bf16[3,8,64,512]{3,2,1,0:T(8,128)(2,1)}, bf16[8,64,512]{2,1,0:T(8,128)(2,1)}) custom-call(bf16[3,8,64,512]{3,2,1,0:T(8,128)(2,1)} %refs_0_.1, s32[8,64,512]{2,1,0:T(8,128)} %refs_1_.1, bf16[8,64,512]{2,1,0:T(8,128)(2,1)} %refs_2_.1, bf16[512,512]{1,0:T(8,128)(2,1)} %constant.24.clone.refs_3_, bf16[512,512]{1,0:T(8,128)(2,1)} %constant.25.clone.refs_4_, ...), custom_call_target="tpu_custom_call" | custom-call | tf_op jit(solution)/shard_map/mixer/pallas_call | solution.py:852
  114.7 2.4 %place.1 = (bf16[3,8,64,512]{3,2,1,0:T(8,128)(2,1)}, bf16[8,64,512]{2,1,0:T(8,128)(2,1)}) custom-call(bf16[3,8,64,512]{3,2,1,0:T(8,128)(2,1)} %get-tuple-element.4.velocity_in, bf16[8,64,512]{2,1,0:T(8,128)(2,1)} %get-tuple-element.5.conc_in), custom_call_target="tpu_custom_call" | custom-call | tf_op jit(solution)/shard_map/place/pallas_call | solution.py:871
